TPU v7x, 128 devices: a whole 4x4x4 slice. The times are simulated.
128 devices in a mesh: group: 4 (over y), shard: 32 (over x, z, core).
Axes of the slice: x: 4, y: 4, z: 4, core: 2. Of those that a mesh axis runs over, the one named last changes fastest.
Arguments:
- queries: bfloat16 [16384, 768], P(('group', 'shard')), may hold values from -12 to 12
- projection: bfloat16 [768, 768], replicated, may hold values from -0.21875 to 0.21875
- labels: bfloat16 [262144, 768], P(('group', 'shard')), may hold values from -6 to 6
- accumulator: float32 [262144], P(('group', 'shard')), may hold values from 0.01 to 4
- shortlist: int32 [16384, 32], P(('group', 'shard')), may hold values from 0 to 1023, all different within a row; in each aligned block of 128 rows (0 to 127, 128 to 255, ...) at most 8 rows name the same one
- positives: int32 [16384, 4], P(('group', 'shard')), may hold values from 0 to 8191
Outputs:
- updated_labels: bfloat16 [262144, 768], P(('group', 'shard'))
- updated_accumulator: float32 [262144], P(('group', 'shard'))
- projection_grad: float32 [768, 768], replicated
Inputs may be any that keep to these rules, and one draw needn't show every extreme that they name: `shortlist`: each query names 32 different clusters. Among the 128 queries of one device no cluster is named more than 8 times, a bound that some block reaches.
All inputs are finite; a program needn't handle non-finite values.
Results may differ from a plain program's by a relative error of at most 0.0036.
The roundings to bfloat16 on the way count: a program that leaves them out, or rounds other values in their place, can miss the bound.
Values may be sent and summed in bfloat16 or wider, within the bound.
A program may use at most 192 MiB of HBM per device.

v0:
```python
import math

import jax
import jax.numpy as jnp
from jax import lax
from jax.sharding import PartitionSpec as P

LBL = 256


learn_rate = 1.0


def slot_select(block_list, block_positives, start, local_clusters, capacity):
    query_rows, short_len = block_list.shape
    cluster_ids = jnp.arange(local_clusters, dtype=jnp.int32)
    picks = ((block_list - start)[:, :, None] == cluster_ids).astype(jnp.bfloat16)
    counts = jnp.sum(picks.astype(jnp.float32), axis=1)
    row_ids = jnp.arange(query_rows, dtype=jnp.int32)
    earlier = (row_ids[:, None] > row_ids[None, :]).astype(jnp.float32)
    prefix = jnp.dot(earlier, counts, precision=lax.Precision.HIGHEST).astype(jnp.bfloat16)
    within = jnp.einsum("qjc,qc->qj", picks, prefix, preferred_element_type=jnp.float32)
    place_ids = jnp.arange(capacity, dtype=jnp.float32)
    places = (within[:, :, None] == place_ids).astype(jnp.bfloat16)
    select = jnp.einsum("qjc,qjw->cwq", picks, places, preferred_element_type=jnp.float32).astype(
        jnp.bfloat16
    )
    column = jnp.arange(short_len, dtype=jnp.int32)
    local_pos = block_positives[:, None, :] - column[None, :, None] * LBL
    inside = (local_pos >= 0) & (local_pos < LBL)
    shifted = jnp.where(inside, local_pos + 1, 0).astype(jnp.bfloat16)
    weighted = places[:, :, :, None] * shifted[:, :, None, :]
    marks = jnp.einsum("qjc,qjwp->cwp", picks, weighted, preferred_element_type=jnp.float32) - 1.0
    return (select, marks.astype(jnp.bfloat16))


def owner_update(row_vectors, target_marks, labels, accumulator, logit_scale):
    local_clusters = row_vectors.shape[0]
    features = row_vectors.shape[2]
    label_slab = labels.reshape(local_clusters, LBL, features)
    scores = (
        jnp.einsum("csd,cld->csl", row_vectors, label_slab, preferred_element_type=jnp.float32)
        * logit_scale
    )
    label_index = jnp.arange(LBL, dtype=jnp.float32)
    target = jnp.any(target_marks.astype(jnp.float32)[..., None] == label_index, axis=2).astype(
        jnp.float32
    )
    signal = (jax.nn.sigmoid(scores) - target).astype(jnp.bfloat16)
    label_grad = (
        jnp.einsum("csl,csd->cld", signal, row_vectors, preferred_element_type=jnp.float32)
        * logit_scale
    )
    new_sums = accumulator.reshape(local_clusters, LBL) + jnp.mean(label_grad * label_grad, axis=2)
    updated = (
        label_slab.astype(jnp.float32) - learn_rate * label_grad / jnp.sqrt(new_sums)[..., None]
    ).astype(jnp.bfloat16)
    query_grad = (
        jnp.einsum("csl,cld->csd", signal, label_slab, preferred_element_type=jnp.float32)
        * logit_scale
    ).astype(jnp.bfloat16)
    return (updated.reshape(-1, features), new_sums.reshape(-1), query_grad)


def deliver(payload, target_marks):
    local_clusters, capacity, features = (payload.shape[1], payload.shape[2], payload.shape[3])
    mark_count = target_marks.shape[3]
    got_payload, got_marks = (
        lax.all_to_all(payload, ("group", "shard"), split_axis=0, concat_axis=2, tiled=True),
        lax.all_to_all(target_marks, ("group", "shard"), split_axis=0, concat_axis=2, tiled=True),
    )
    return (
        got_payload.reshape(local_clusters, -1, features),
        got_marks.reshape(local_clusters, -1, mark_count),
    )


def bring_back(query_grad, groups, shards, capacity):
    local_clusters, features = (query_grad.shape[0], query_grad.shape[2])
    returned = lax.all_to_all(
        query_grad.reshape(1, local_clusters, groups * shards * capacity, features),
        ("group", "shard"),
        split_axis=2,
        concat_axis=0,
        tiled=True,
    )
    return returned.reshape(-1, capacity, features)


def on_device(queries, projection, labels, accumulator, shortlist, positives):
    query_rows, features = queries.shape
    short_len = shortlist.shape[1]
    mark_count = positives.shape[1]
    groups = lax.axis_size("group")
    shards = lax.axis_size("shard")
    devices = groups * shards
    local_clusters = labels.shape[0] // LBL
    clusters = local_clusters * devices
    capacity = 2 * query_rows * short_len // clusters
    logit_scale = 1.0 / math.sqrt(features)
    select, marks = slot_select(shortlist, positives, 0, clusters, capacity)
    target_marks = marks.reshape(devices, local_clusters, capacity, mark_count)
    hidden = jnp.dot(queries, projection, preferred_element_type=jnp.float32).astype(jnp.bfloat16)
    payload = jnp.einsum("cwq,qd->cwd", select, hidden, preferred_element_type=jnp.float32).astype(
        jnp.bfloat16
    )
    payload = payload.reshape(devices, local_clusters, capacity, features)
    row_vectors, got_marks = deliver(payload, target_marks)
    updated, new_sums, query_grad = owner_update(
        row_vectors, got_marks, labels, accumulator, logit_scale
    )
    returned = bring_back(query_grad, groups, shards, capacity)
    summed = jnp.einsum("cwq,cwd->qd", select, returned, preferred_element_type=jnp.float32)
    partial_grad = jnp.dot(queries.astype(jnp.float32).T, summed, precision=lax.Precision.HIGHEST)
    summed_grad = lax.psum(partial_grad, ("group", "shard"))
    factor = jnp.minimum(1.0, features / jnp.sqrt(jnp.sum(summed_grad * summed_grad) + 1e-06))
    return (updated, new_sums, summed_grad * factor)


def solution(mesh):
    in_specs = (
        P(("group", "shard"), None),
        P(),
        P(("group", "shard"), None),
        P(("group", "shard")),
        P(("group", "shard"), None),
        P(("group", "shard"), None),
    )
    out_specs = (P(("group", "shard"), None), P(("group", "shard")), P())
    return jax.shard_map(
        on_device, mesh=mesh, in_specs=in_specs, out_specs=out_specs, check_vma=False
    )
```

profile of v0, /device:TPU:1, one launch (start us, length us, event | category | flops | bytes accessed | tf_op | source)
XLA Modules:
  0.0 660.4 jit_solution(13768900425391218592)
XLA Ops:
  7.2 0.0 copy-start
  7.2 2.8 convert_reduce_fusion
  10.0 3.4 iota_compare_fusion.1
  13.4 0.4 fusion.21
  13.8 0.0 copy-start.8
  13.8 8.1 %fusion.3 = f32[128,1,32]{2,1,0:T(1,128)S(1)} fusion(pred[128,32,1024]{2,0,1:T(32,128)(4,1)S(1)} %iota_compare_fusion.1, bf16[128,1024,1]{1,0,2:T(8,128)(2,1)S(1)} %fusion.21), kind=kOutput, calls=%fused_computation.7 | convolution fusion | flops 8388608 | bytes 4472832 | tf_op jit(solution)/shard_map/qjc,qc->qj/dot_general | solution.py:22
  22.0 0.6 copy-done.6
  22.6 0.1 fusion.32
  22.7 0.2 copy.54
  22.9 0.1 fusion.39
  23.0 2.7 fusion.29
  25.7 1.2 reshape.78
  26.9 0.9 copy.96
  27.8 1.7 reshape.92
  29.5 11.5 %all-to-all-start.1 = ((bf16[128,2,128]{2,1,0:T(2,128)(2,1)}), bf16[128,2,128]{2,1,0:T(2,128)(2,1)S(1)}, u32[]{:S(2)}, u32[]{:S(2)}) async-start(bf16[128,2,128]{2,1,0:T(2,128)(2,1)} %reshape.92), calls=%async_computation.1 | async-start | bytes 131072 | tf_op jit(solution)/shard_map/all_to_all | solution.py:70
  41.1 0.0 copy-start.4
  41.1 12.6 %convert_bitcast_fusion.2 = bf16[1024,8,128]{0,1,2:T(8,128)(2,1)S(1)} fusion(pred[128,32,1024]{2,0,1:T(32,128)(4,1)} %copy-done.3, f32[128,32]{1,0:T(8,128)} %bitcast.92), kind=kOutput, calls=%fused_computation.28 | convolution fusion | flops 68190208 | bytes 6307840 | tf_op jit(solution)/shard_map/qjc,qjw->cwq/dot_general | solution.py:25
  53.7 9.3 %convert_bitcast_fusion = bf16[128,8,8,768]{3,1,0,2:T(8,128)(2,1)} fusion(bf16[1024,8,128]{0,1,2:T(8,128)(2,1)S(1)} %convert_bitcast_fusion.2, bf16[128,768]{1,0:T(8,128)(2,1)S(1)} %copy-done.4, bf16[768,768]{1,0:T(8,128)(2,1)S(1)} %copy-done), kind=kOutput, calls=%fused_computation.17 | convolution fusion | flops 1767997440 | bytes 16056320 | tf_op jit(solution)/shard_map/cwq,qd->cwd/dot_general | solution.py:104
  63.0 11.0 %copy.52 = bf16[128,8,8,768]{3,1,2,0:T(8,128)(2,1)} copy(bf16[128,8,8,768]{3,1,0,2:T(8,128)(2,1)} %convert_bitcast_fusion) | data formatting | bytes 25165824 | tf_op jit(solution)/shard_map/reshape | solution.py:107
  74.0 19.9 %all-to-all-start = ((bf16[128,8,8,768]{3,1,2,0:T(8,128)(2,1)}), bf16[128,8,8,768]{3,1,2,0:T(8,128)(2,1)}, u32[]{:S(2)}, u32[]{:S(2)}) async-start(bf16[128,8,8,768]{3,1,2,0:T(8,128)(2,1)} %copy.52), calls=%async_computation | async-start | bytes 25165824 | tf_op jit(solution)/shard_map/all_to_all | solution.py:69
  93.9 1.2 reshape.93
  95.1 1.6 convert_bitcast_fusion.1
  96.7 3.4 copy.68
  100.2 2.7 reshape.91
  102.9 7.4 %fusion = pred[8,1024,256]{2,1,0:T(8,128)(4,1)} fusion(f32[8,1024,4]{1,2,0:T(4,128)S(1)} %reshape.91), kind=kLoop, calls=%fused_computation.1 | loop fusion | flops 14680064 | bytes 2228224 | tf_op jit(solution)/shard_map/reduce_or | solution.py:46
  110.3 145.1 %all-to-all-done = bf16[128,8,8,768]{3,1,2,0:T(8,128)(2,1)} async-done(((bf16[128,8,8,768]{3,1,2,0:T(8,128)(2,1)}), bf16[128,8,8,768]{3,1,2,0:T(8,128)(2,1)}, u32[]{:S(2)}, u32[]{:S(2)}) %all-to-all-start) | async-done | bytes 12582944 | tf_op jit(solution)/shard_map/all_to_all | solution.py:69
  255.4 11.4 %subtract_convert_fusion = bf16[8,1024,256]{2,1,0:T(8,128)(2,1)} fusion(pred[8,1024,256]{2,1,0:T(8,128)(4,1)} %fusion, bf16[8,256,768]{2,1,0:T(8,128)(2,1)} %bitcast.87, bf16[1,8,128,8,768]{4,1,3,2,0:T(8,128)(2,1)} %bitcast.8), kind=kOutput, calls=%fused_computation.21 | convolution fusion | flops 3235905536 | bytes 22020096 | tf_op jit(solution)/shard_map/csd,cld->csl/dot_general | solution.py:42
  266.8 11.2 %fusion.7 = bf16[1,8,1024,768]{3,2,1,0:T(8,128)(2,1)} fusion(bf16[8,1024,256]{2,1,0:T(8,128)(2,1)} %subtract_convert_fusion, bf16[8,256,768]{2,1,0:T(8,128)(2,1)} %bitcast.88), kind=kOutput, calls=%fused_computation.11 | convolution fusion | flops 3233808384 | bytes 19922944 | tf_op jit(solution)/shard_map/csl,cld->csd/dot_general | solution.py:59
  278.0 14.2 %copy.59 = bf16[1,8,1024,768]{3,1,0,2:T(8,128)(2,1)} copy(bf16[1,8,1024,768]{3,2,1,0:T(8,128)(2,1)} %fusion.7) | data formatting | bytes 25165824 | tf_op jit(solution)/shard_map/reshape | solution.py:81
  292.2 13.2 %all-to-all-start.2 = ((bf16[1,8,1024,768]{3,1,0,2:T(8,128)(2,1)}), bf16[1,8,1024,768]{3,1,0,2:T(8,128)(2,1)}, u32[]{:S(2)}, u32[]{:S(2)}) async-start(bf16[1,8,1024,768]{3,1,0,2:T(8,128)(2,1)} %copy.59), calls=%async_computation.2 | async-start | bytes 25165824 | tf_op jit(solution)/shard_map/all_to_all | solution.py:80
  305.4 0.0 copy-start.7
  305.4 0.0 all-reduce.2.cloned.1.call-start
  305.4 3.4 copy.62
  308.9 13.0 %multiply_reduce_fusion = (f32[8,256]{1,0:T(8,128)S(1)}, f32[8,256,768]{2,1,0:T(8,128)}) fusion(bf16[8,1024,256]{2,1,0:T(8,128)(2,1)} %subtract_convert_fusion, bf16[1,8,128,8,768]{4,1,3,2,0:T(8,128)(2,1)} %bitcast.8), kind=kOutput, calls=%fused_computation.24 | convolution fusion | flops 3225942016 | bytes 23076864 | tf_op jit(solution)/shard_map/csl,csd->cld/dot_general | solution.py:51
  321.8 145.4 %all-to-all-done.2 = bf16[1,8,1024,768]{3,1,0,2:T(8,128)(2,1)} async-done(((bf16[1,8,1024,768]{3,1,0,2:T(8,128)(2,1)}), bf16[1,8,1024,768]{3,1,0,2:T(8,128)(2,1)}, u32[]{:S(2)}, u32[]{:S(2)}) %all-to-all-start.2) | async-done | bytes 12582944 | tf_op jit(solution)/shard_map/all_to_all | solution.py:80
  467.3 7.9 %copy.95 = bf16[1,8,1024,768]{3,2,1,0:T(8,128)(2,1)S(1)} copy(bf16[1,8,1024,768]{3,1,0,2:T(8,128)(2,1)} %all-to-all-done.2) | data formatting | bytes 25165824 | tf_op jit(solution)/shard_map/all_to_all | solution.py:80
  475.2 0.0 copy-start.2
  475.2 5.9 copy.61
  481.1 6.5 convolution_bitcast_fusion.1
  487.6 2.5 convolution_bitcast_fusion
  490.2 0.0 all-reduce.2.cloned.1.call-update
  490.2 0.6 add.33
  490.8 5.5 subtract_convert_fusion.1
  496.3 149.3 %all-reduce.2.cloned.1.call-done = f32[768,768]{0,1:T(8,128)} async-done(((f32[768,768]{0,1:T(8,128)}), f32[768,768]{0,1:T(8,128)}) %all-reduce.2.cloned.1.call-update) | async-done | bytes 2359312 | tf_op jit(solution)/shard_map/psum | solution.py:115
  645.7 2.9 multiply_reduce_fusion.1
  649.3 0.0 copy-start.1
  649.3 1.9 broadcast_multiply_fusion
  651.2 2.0 copy.63
  (16 shorter events, 0.0 us)
Async XLA Ops:
  7.2 46.5 %copy-start = (bf16[768,768]{1,0:T(8,128)(2,1)S(1)}, bf16[768,768]{1,0:T(8,128)(2,1)}, u32[]{:S(2)}) copy-start(bf16[768,768]{1,0:T(8,128)(2,1)} %param.7) | copy-start | bytes 3538948
  13.4 8.6 %copy-start.3 = (pred[128,32,1024]{2,0,1:T(32,128)(4,1)}, pred[128,32,1024]{2,0,1:T(32,128)(4,1)S(1)}, u32[]{:S(2)}) copy-start(pred[128,32,1024]{2,0,1:T(32,128)(4,1)S(1)} %iota_compare_fusion.1) | copy-start | bytes 12582916
  13.8 9.1 %copy-start.8 = (s32[128,4]{0,1:T(4,128)S(1)}, s32[128,4]{0,1:T(4,128)}, u32[]{:S(2)}) copy-start(s32[128,4]{0,1:T(4,128)} %param.11) | copy-start | bytes 6148
  13.8 9.2 %copy-start.5 = (s32[128,32]{0,1:T(8,128)S(1)}, s32[128,32]{0,1:T(8,128)}, u32[]{:S(2)}) copy-start(s32[128,32]{0,1:T(8,128)} %param.10) | copy-start | bytes 49156
  22.0 0.6 copy-start.6
  29.5 44.5 %all-to-all-start.1 = ((bf16[128,2,128]{2,1,0:T(2,128)(2,1)}), bf16[128,2,128]{2,1,0:T(2,128)(2,1)S(1)}, u32[]{:S(2)}, u32[]{:S(2)}) async-start(bf16[128,2,128]{2,1,0:T(2,128)(2,1)} %reshape.92), calls=%async_computation.1 | async-start | bytes 131072 | tf_op jit(solution)/shard_map/all_to_all | solution.py:70
  41.1 12.6 %copy-start.4 = (bf16[128,768]{1,0:T(8,128)(2,1)S(1)}, bf16[128,768]{1,0:T(8,128)(2,1)}, u32[]{:S(2)}) copy-start(bf16[128,768]{1,0:T(8,128)(2,1)} %param.6) | copy-start | bytes 589828
  74.0 181.4 %all-to-all-start = ((bf16[128,8,8,768]{3,1,2,0:T(8,128)(2,1)}), bf16[128,8,8,768]{3,1,2,0:T(8,128)(2,1)}, u32[]{:S(2)}, u32[]{:S(2)}) async-start(bf16[128,8,8,768]{3,1,2,0:T(8,128)(2,1)} %copy.52), calls=%async_computation | async-start | bytes 25165824 | tf_op jit(solution)/shard_map/all_to_all | solution.py:69
  292.2 175.1 %all-to-all-start.2 = ((bf16[1,8,1024,768]{3,1,0,2:T(8,128)(2,1)}), bf16[1,8,1024,768]{3,1,0,2:T(8,128)(2,1)}, u32[]{:S(2)}, u32[]{:S(2)}) async-start(bf16[1,8,1024,768]{3,1,0,2:T(8,128)(2,1)} %copy.59), calls=%async_computation.2 | async-start | bytes 25165824 | tf_op jit(solution)/shard_map/all_to_all | solution.py:80
  305.4 3.5 copy-start.7
  305.4 340.3 %all-reduce.2.cloned.1.call-start = ((), (), s32[]{:S(2)}) async-start(), calls=%async_computation.3 | async-start | bytes 4718592 | tf_op jit(solution)/shard_map/psum | solution.py:115
  475.2 5.9 copy-start.2
  649.3 3.9 copy-start.1
Sparse Core Ops, SparseCore 0:
  490.3 155.3 all-reduce.1
where the time goes:
time: 670 us; the launch traced here: 660 us
  waiting for transfers between devices  440 us (66%)
  matrix products  77.8 us (12%)
  local copies, waits for them, and re-layouts  56.4 us (8%)
  starting transfers between devices  44.7 us (7%)
  other arithmetic  26.3 us (4%)
  between operations  15.3 us (2%)
    psum x1, waiting for transfers between devices, on_device(): summed_grad = lax.psum(partial_grad, ('group', 'shard'))  149 us
    all_to_all x1, waiting for transfers between devices, bring_back(): lax.all_to_all(query_grad.reshape(1, local_clusters, groups * shards * ca...  145 us
    all_to_all x1, waiting for transfers between devices, deliver(): lax.all_to_all(payload, ('group', 'shard'), split_axis=0, concat_axis=2,...  145 us
    all_to_all x1, starting transfers between devices, deliver(): lax.all_to_all(payload, ('group', 'shard'), split_axis=0, concat_axis=2,...  19.9 us
    reshape x1, local copies, waits for them, and re-layouts, bring_back(): query_grad.reshape(1, local_clusters, groups * shards * capacity, features)  14.2 us
    all_to_all x2, local copies, waits for them, and re-layouts, bring_back(): lax.all_to_all(query_grad.reshape(1, local_clusters, groups * shards * ca...  13.8 us
  transfers between devices with their start and end apart: 4, of which 3 were waited for; matrix products, arithmetic and copies ran while one was open for 11% of the time, Pallas kernels for 0%

commit v1 on v0

v1 whole, which is shorter than its diff:
```python
import functools
import math

import jax
import jax.numpy as jnp
from jax import lax
from jax.experimental import pallas as pl
from jax.experimental.pallas import tpu as pltpu
from jax.sharding import PartitionSpec as P

MESH = pl.DeviceIdType.MESH
LBL = 256
QD = 128
D = 768
CL = 8
W = 8
BF = jnp.bfloat16
F32 = jnp.float32
ORDERS = ((0, 1, 2), (1, 2, 0), (2, 0, 1))
OFF = (0, -1, 1, 2)
GROUP = 16


def arrival(offset):
    place = {0: 0, 3: 1, 1: 2, 2: 3}
    worst = 0
    for order in ORDERS:
        third, second = place[offset[order[2]]], place[offset[order[1]]]
        if third == 0:
            tick = (0, 1, 1, 2)[second]
        else:
            tick = (3 + second) if third in (1, 2) else 4 + second
        worst = max(worst, tick)
    return worst


CHIPS = sorted(
    [(a, b, c) for a in range(4) for b in range(4) for c in range(4)],
    key=lambda o: (arrival(o), o),
)


def dot(a, b, ca=1, cb=0):
    return lax.dot_general(a, b, (((ca,), (cb,)), ((), ())), preferred_element_type=F32)


def split(value):
    high = value.astype(BF)
    return high, (value - high.astype(F32)).astype(BF)


def kernel(
    q_ref, meta_ref, p_ref, tri_ref, acc_ref, l_hbm,
    new_hbm, sums_ref, proj_ref,
    gq, gm, lab, lp, lt, total, rows, cp, cd, mk, mc, pj, rb0, rb1, rb2, rb3, s1, s2, g1, full, stage,
    sem_l, sem_o,
    qs, qr, ms, mr, bs, br, bms, bmr, rs, rr,
):
    y = lax.axis_index("group")
    s = lax.axis_index("shard")
    x, z, k = s // 8, (s // 2) % 4, s % 2
    here = (x, y, z)
    scale = 1.0 / math.sqrt(D)

    def device(c, core):
        return (c[1], (c[0] * 4 + c[2]) * 2 + core)

    def shifted(axis, r):
        c = list(here)
        c[axis] = (c[axis] + r + 4) % 4
        return device(c, k)

    sibling = device(here, 1 - k)

    pending = []

    def remote(src, dst, ssem, rsem, target):
        copy = pltpu.make_async_remote_copy(
            src_ref=src, dst_ref=dst, send_sem=ssem, recv_sem=rsem,
            device_id=target, device_id_type=MESH,
        )
        copy.start()
        pending.append((src, ssem))

    def arrived(dst, rsem):
        pltpu.make_async_remote_copy(
            src_ref=dst, dst_ref=dst, send_sem=rsem, recv_sem=rsem,
            device_id=sibling, device_id_type=MESH,
        ).wait_recv()

    barrier = pltpu.get_barrier_semaphore()
    for axis in range(3):
        for r in (1, 2, 3):
            pl.semaphore_signal(barrier, inc=1, device_id=shifted(axis, r), device_id_type=MESH)
    pl.semaphore_signal(barrier, inc=1, device_id=sibling, device_id_type=MESH)
    pl.semaphore_wait(barrier, 10)

    load = pltpu.make_async_copy(l_hbm, lab, sem_l)
    load.start()

    at = [[here[a] for a in order] for order in ORDERS]

    def near(t, phase, i):
        return (at[t][phase] + OFF[i] + 4) % 4

    for t in range(3):
        i1, i2, i3 = at[t]
        gm[t, k, i3, i2, i1] = meta_ref[t]
        gq[t, k, i3, i2, i1] = q_ref[:, t * 256:(t + 1) * 256]

    def meta_phase(t, phase, ref):
        for r in (1, 2, 3):
            remote(ref, ref, ms.at[t, phase, r - 1], mr.at[t, phase, r - 1], shifted(ORDERS[t][phase], r))

    def meta_wait(t, phase, ref_of):
        for r in (1, 2, 3):
            arrived(ref_of((at[t][phase] - r + 4) % 4), mr.at[t, phase, r - 1])

    def both_ways(t, phase, n, ref):
        for way, r in ((0, 1), (1, -1)):
            remote(ref, ref, qs.at[t, n, way], qr.at[t, n, way], shifted(ORDERS[t][phase], r))

    def onward(t, phase, n, way, ref, half):
        arrived(ref, qr.at[t, n, way])
        part = half(ref, way)
        r = 1 if way == 0 else -1
        remote(part, part, qs.at[t, n + 1, way], qr.at[t, n + 1, way], shifted(ORDERS[t][phase], r))

    def far(t, n, ref, half):
        for way in (0, 1):
            arrived(half(ref, way), qr.at[t, n + 1, way])

    def row_half(ref, way):
        return ref.at[pl.ds(64 * way, 64)]

    def line_half(ref, way):
        return ref.at[pl.ds(2 * way, 2)]

    def line(t, r3, j):
        return gq.at[t, k, near(t, 2, r3), near(t, 1, j)]

    def to_sibling(t, r3, j):
        ref = line(t, r3, j)
        remote(ref, ref, bs.at[t, r3, j], br.at[t, r3, j], sibling)

    def from_sibling(t, r3, j):
        arrived(gq.at[t, 1 - k, near(t, 2, r3), near(t, 1, j)], br.at[t, r3, j])

    T3 = range(3)
    for t in T3:
        i1, i2, i3 = at[t]
        meta_phase(t, 0, gm.at[t, k, i3, i2, i1])
    for t in T3:
        i1, i2, i3 = at[t]
        both_ways(t, 0, 0, gq.at[t, k, i3, i2, i1])

    load.wait()

    def prepare(c, _):
        here_l = pl.ds(pl.multiple_of(c * LBL, LBL), LBL)
        slab = lab[here_l, :]
        lp[here_l, :] = dot(slab, p_ref[...], 1, 1).astype(BF)
        lt[:, here_l] = slab.T
        return 0

    for t in T3:
        i1, i2, i3 = at[t]
        onward(t, 0, 0, 0, gq.at[t, k, i3, i2, near(t, 0, 1)], row_half)
        onward(t, 0, 0, 1, gq.at[t, k, i3, i2, near(t, 0, 2)], row_half)
    for t in T3:
        i1, i2, i3 = at[t]
        meta_wait(t, 0, lambda i: gm.at[t, k, i3, i2, i])
        meta_phase(t, 1, gm.at[t, k, i3, i2])
    for t in T3:
        i1, i2, i3 = at[t]
        far(t, 0, gq.at[t, k, i3, i2, near(t, 0, 3)], row_half)
        both_ways(t, 1, 2, line(t, 0, 0))
        both_ways(t, 2, 4, line(t, 0, 0))
        to_sibling(t, 0, 0)
    lax.fori_loop(0, 2, prepare, 0)
    for t in T3:
        i1, i2, i3 = at[t]
        meta_wait(t, 1, lambda i: gm.at[t, k, i3, i])
        meta_phase(t, 2, gm.at[t, k, i3])
        remote(gm.at[t, k, i3], gm.at[t, k, i3], bms.at[t, 0], bmr.at[t, 0], sibling)
    lax.fori_loop(2, 4, prepare, 0)
    for way in (0, 1):
        for t in T3:
            j = way + 1
            onward(t, 1, 2, way, line(t, 0, j), line_half)
            both_ways(t, 2, 4 + 2 * j, line(t, 0, j))
            to_sibling(t, 0, j)
    lax.fori_loop(4, 6, prepare, 0)
    for t in T3:
        far(t, 2, line(t, 0, 3), line_half)
        both_ways(t, 2, 10, line(t, 0, 3))
        to_sibling(t, 0, 3)
    for t in T3:
        meta_wait(t, 2, lambda i: gm.at[t, k, i])
        for r in (1, 2, 3):
            ref = gm.at[t, k, (at[t][2] + r) % 4]
            remote(ref, ref, bms.at[t, r], bmr.at[t, r], sibling)
    lax.fori_loop(6, 8, prepare, 0)
    total[...] = jnp.zeros_like(total)
    for t in T3:
        for r in range(4):
            arrived(gm.at[t, 1 - k, (at[t][2] + r) % 4], bmr.at[t, r])

    number = y * 32 + s
    first = number * CL
    octave = first // 128
    base = (128 + first % 128).astype(F32)
    power = lax.shift_left(jnp.int32(1), octave.astype(jnp.int32)).astype(F32)

    def place_of(group, i):
        words = []
        for h in range(4):
            word = 0
            for n in range(4):
                o = CHIPS[group * GROUP + h * 4 + n]
                word |= (o[0] + 4 * o[1] + 16 * o[2]) << (6 * n)
            words.append(word)
        h, n = i // 4, i % 4
        word = jnp.where(h == 0, words[0], jnp.where(h == 1, words[1], jnp.where(h == 2, words[2], words[3])))
        code = lax.shift_right_logical(word.astype(jnp.int32), (6 * n).astype(jnp.int32))
        cx, cy, cz = code % 4, (code // 4) % 4, (code // 16) % 4
        return ((x + cx) % 4, (y + cy) % 4, (z + cz) % 4)

    def indices(c, t):
        a1, a2, a3 = ORDERS[t]
        return c[a3], c[a2], c[a1]

    def pair(ref, c, t):
        n3, n2, n1 = indices(c, t)
        return ref[t, 0, n3, n2, n1], ref[t, 1, n3, n2, n1]

    lane = lax.broadcasted_iota(jnp.int32, (16, 256), 1)
    sub = lax.broadcasted_iota(jnp.int32, (16, 256), 0)
    own_slot = jnp.where(sub // W == lane // QD, sub % W, -2).astype(F32)
    own_cluster = (
        lax.broadcasted_iota(jnp.int32, (CL, 128), 0) == lax.broadcasted_iota(jnp.int32, (CL, 128), 1) // 16
    )
    lane_chip = lax.broadcasted_iota(jnp.int32, (8, 128), 1) // 16

    def group_work(group):
        def names(i, _):
            c = place_of(group, i)
            a0, a1 = pair(gm, c, 0)
            b0, b1 = pair(gm, c, 1)
            ids = jnp.concatenate(
                [jnp.concatenate([a0, b0], axis=0), jnp.concatenate([a1, b1], axis=0)], axis=1
            ).astype(F32)
            column = lax.broadcasted_iota(jnp.int32, (32, 256), 0).astype(F32) + 1.0
            found = []
            for n in range(CL):
                found.append(jnp.sum(jnp.where(ids == (base + n) * power, column, 0.0), axis=0, keepdims=True))
            cp[pl.ds(pl.multiple_of(i * CL, CL), CL), :] = jnp.concatenate(found, axis=0)
            return 0

        lax.fori_loop(0, GROUP, names, 0)
        picked = cp[...] > 0.0
        rank = dot(jnp.where(picked, 1.0, 0.0).astype(BF), tri_ref[...])
        cd[...] = jnp.where(picked, rank, -1.0)

        def choose(i, _):
            c = place_of(group, i)
            here_c = pl.ds(pl.multiple_of(i * CL, CL), CL)
            code = cd[here_c, :]
            onehot = jnp.concatenate(
                [jnp.where(code[n:n + 1, :] == own_slot, 1.0, 0.0).astype(BF) for n in range(CL)], axis=0
            )
            m0, m1 = pair(gm, c, 2)
            marks = jnp.concatenate([m0, m1], axis=1).astype(F32)
            column = cp[here_c, :]
            shifted_marks = jnp.concatenate(
                [jnp.where(marks[n:n + 1, :] == column, marks[4 + n:5 + n, :], 0.0) for n in range(4)], axis=0
            ).astype(BF)
            spread = dot(shifted_marks, onehot, 1, 1)
            mk[i] = jnp.concatenate(
                [
                    jnp.sum(jnp.where(own_cluster, spread[n * CL:(n + 1) * CL, :], 0.0), axis=0, keepdims=True)
                    for n in range(4)
                ]
                + [jnp.zeros((4, 128), F32)],
                axis=0,
            )
            at_row = pl.ds(pl.multiple_of(i * 16, 16), 16)
            for t in T3:
                q0, q1 = pair(gq, c, t)
                got = dot(onehot, jnp.concatenate([q0, q1], axis=0)).astype(BF)
                for n in range(CL):
                    rows[n, at_row, t * 256:(t + 1) * 256] = got[n * 16:(n + 1) * 16, :]
            return 0

        lax.fori_loop(0, GROUP, choose, 0)
        for h in range(GROUP // 8):
            for n in range(CL):
                line_marks = jnp.zeros((8, 128), F32)
                for i in range(8):
                    turned = pltpu.roll(mk[h * 8 + i], (16 * (i - n)) % 128, 1)
                    line_marks = jnp.where(lane_chip == i, turned, line_marks)
                mc[n, :, h * 128:(h + 1) * 128] = line_marks

        def cluster(n, _):
            here_l = pl.ds(pl.multiple_of(n * LBL, LBL), LBL)
            r = rows[n]
            scores = dot(lp[here_l, :], r, 1, 1) * scale
            label = lax.broadcasted_iota(jnp.int32, (LBL, GROUP * 16), 0).astype(F32) + 1.0
            m = mc[n]
            hit = (m[0:1] == label) | (m[1:2] == label) | (m[2:3] == label) | (m[3:4] == label)
            signal = 1.0 / (1.0 + jnp.exp(-scores)) - jnp.where(hit, 1.0, 0.0)
            total[here_l, :] += dot(signal.astype(BF), r)
            return 0

        lax.fori_loop(0, CL, cluster, 0)

    def lines_after(j):
        for way in (0, 1):
            for t in T3:
                onward(t, 2, 4 + 2 * j, way, line(t, 1 + way, j), line_half)
                to_sibling(t, 1 + way, j)

    def far_after(j):
        for t in T3:
            far(t, 4 + 2 * j, line(t, 3, j), line_half)
            to_sibling(t, 3, j)

    def sibling_after(r3s, j):
        for t in T3:
            for r3 in r3s:
                from_sibling(t, r3, j)

    sibling_after((0,), 0)
    sibling_after((0,), 1)
    sibling_after((0,), 2)
    sibling_after((0,), 3)
    lines_after(0)
    lines_after(1)
    far_after(0)
    sibling_after((1, 2), 0)
    sibling_after((1, 2), 1)
    sibling_after((3,), 0)
    group_work(0)
    lines_after(2)
    far_after(1)
    sibling_after((1, 2), 2)
    sibling_after((3,), 1)
    group_work(1)
    lines_after(3)
    far_after(2)
    sibling_after((1, 2), 3)
    sibling_after((3,), 2)
    group_work(2)
    far_after(3)
    sibling_after((3,), 3)
    group_work(3)

    def project(half):
        at_half = pl.ds(pl.multiple_of(half * 384, 128), 384)

        def step(n, _):
            here_l = pl.ds(pl.multiple_of(n * LBL, LBL), LBL)
            high, low = split(total[here_l, :])
            left = lt[at_half, here_l]
            add = dot(left, high) + dot(left, low)
            pj[at_half, :] = jnp.where(n == 0, add, pj[at_half, :] + add)
            return 0

        lax.fori_loop(0, CL, step, 0)

    other_half = pl.ds(pl.multiple_of((1 - k) * 384, 128), 384)
    own_half = pl.ds(pl.multiple_of(k * 384, 128), 384)
    project(1 - k)
    remote(pj.at[other_half], rb0, rs.at[0], rr.at[0], sibling)
    project(k)

    eye = lax.broadcasted_iota(jnp.int32, (128, 128), 0) == lax.broadcasted_iota(jnp.int32, (128, 128), 1)

    def adagrad(n, _):
        here_l = pl.ds(pl.multiple_of(n * LBL, LBL), LBL)
        high, low = split(total[here_l, :])
        grad = (dot(high, p_ref[...]) + dot(low, p_ref[...])) * scale
        mean = jnp.sum(grad * grad, axis=1, keepdims=True) * (1.0 / D)
        old = jnp.concatenate(
            [
                jnp.sum(jnp.where(eye, acc_ref[pl.ds(n * 2 + h, 1), :], 0.0), axis=1, keepdims=True)
                for h in range(2)
            ],
            axis=0,
        )
        sums = old + mean
        for h in range(2):
            sums_ref[pl.ds(n * 2 + h, 1), :] = jnp.sum(
                jnp.where(eye, sums[h * 128:(h + 1) * 128], 0.0), axis=0, keepdims=True
            )
        stage[here_l, :] = (lab[here_l, :].astype(F32) - grad * (1.0 / jnp.sqrt(sums))).astype(BF)
        return 0

    lax.fori_loop(0, 1, adagrad, 0)
    arrived(rb0, rr.at[0])
    pj[own_half, :] += rb0[...]

    def cols(t):
        return pl.ds(t * 256, 256)

    def exchange(n, t, phase, src_of, dst_of):
        for r in (1, 2, 3):
            slot = 1 + n * 9 + t * 3 + r - 1
            remote(src_of(r), dst_of(r), rs.at[slot], rr.at[slot], shifted(ORDERS[t][phase], r))

    def exchanged(n, t, phase, dst_of):
        for r in (1, 2, 3):
            slot = 1 + n * 9 + t * 3 + r - 1
            arrived(dst_of(r, (at[t][phase] - r + 4) % 4), rr.at[slot])

    def piece(i):
        return pl.ds(pl.multiple_of(k * 384 + i * 96, 32), 96)

    for t in T3:
        exchange(0, t, 0, lambda r: pj.at[piece((at[t][0] + r) % 4), cols(t)], lambda r: rb1.at[t, r - 1])
    lax.fori_loop(1, 4, adagrad, 0)
    for t in T3:
        exchanged(0, t, 0, lambda r, i: rb1.at[t, r - 1])
        s1[t] = pj[piece(at[t][0]), cols(t)] + rb1[t, 0] + rb1[t, 1] + rb1[t, 2]
        exchange(
            1, t, 1,
            lambda r: s1.at[t, pl.ds(pl.multiple_of((at[t][1] + r) % 4 * 24, 8), 24)],
            lambda r: rb2.at[t, r - 1],
        )
    lax.fori_loop(4, 5, adagrad, 0)
    for t in T3:
        exchanged(1, t, 1, lambda r, i: rb2.at[t, r - 1])
        s2[t] = s1[t, pl.ds(pl.multiple_of(at[t][1] * 24, 8), 24)] + rb2[t, 0] + rb2[t, 1] + rb2[t, 2]
        rb3[t, at[t][2]] = s2[t]
        exchange(2, t, 2, lambda r: s2.at[t], lambda r: rb3.at[t, at[t][2]])
    lax.fori_loop(5, 6, adagrad, 0)
    for t in T3:
        exchanged(2, t, 2, lambda r, i: rb3.at[t, i])
        mine = pl.ds(pl.multiple_of(at[t][1] * 24, 8), 24)
        g1[t, mine] = (rb3[t, 0] + rb3[t, 1]) + (rb3[t, 2] + rb3[t, 3])
        exchange(3, t, 1, lambda r: g1.at[t, mine], lambda r: g1.at[t, mine])
    lax.fori_loop(6, 7, adagrad, 0)
    for t in T3:
        exchanged(3, t, 1, lambda r, i: g1.at[t, pl.ds(pl.multiple_of(i * 24, 8), 24)])
        full[piece(at[t][0]), cols(t)] = g1[t]
        exchange(4, t, 0, lambda r: g1.at[t], lambda r: full.at[piece(at[t][0]), cols(t)])
    lax.fori_loop(7, 8, adagrad, 0)
    store = pltpu.make_async_copy(stage, new_hbm, sem_o)
    store.start()
    for t in T3:
        exchanged(4, t, 0, lambda r, i: full.at[piece(i), cols(t)])
    remote(full.at[own_half], full.at[own_half], rs.at[46], rr.at[46], sibling)
    arrived(full.at[other_half], rr.at[46])

    squares = jnp.sum(full[...] * full[...]) * (scale * scale)
    factor = jnp.minimum(1.0, D / jnp.sqrt(squares + 1e-06)) * scale
    proj_ref[...] = full[...] * factor

    store.wait()
    for src, ssem in pending:
        pltpu.make_async_remote_copy(
            src_ref=src, dst_ref=src, send_sem=ssem, recv_sem=ssem,
            device_id=sibling, device_id_type=MESH,
        ).wait_send()


def on_device(queries, projection, labels, accumulator, shortlist, positives):
    ids = shortlist.astype(jnp.int32)
    codes = lax.shift_left(128 + ids % 128, ids // 128).T
    marks = jnp.concatenate([positives // LBL + 1, positives % LBL + 1], axis=1).T
    meta = jnp.concatenate([codes, marks, jnp.zeros((8, QD), jnp.int32)], axis=0).astype(BF).reshape(3, 16, QD)
    ordinal = jnp.arange(2 * QD)
    tri = (
        (ordinal[:, None] < ordinal[None, :]) & (ordinal[:, None] // QD == ordinal[None, :] // QD)
    ).astype(BF)
    vmem = pl.BlockSpec(memory_space=pltpu.VMEM)
    hbm = pl.BlockSpec(memory_space=pl.ANY)
    dma = pltpu.SemaphoreType.DMA
    new_labels, sums, proj = pl.pallas_call(
        kernel,
        out_shape=(
            jax.ShapeDtypeStruct((CL * LBL, D), BF),
            jax.ShapeDtypeStruct((16, 128), F32),
            jax.ShapeDtypeStruct((D, D), F32),
        ),
        in_specs=[vmem] * 5 + [hbm],
        out_specs=(hbm, vmem, vmem),
        scratch_shapes=[
            pltpu.VMEM((3, 2, 4, 4, 4, QD, 256), BF),
            pltpu.VMEM((3, 2, 4, 4, 4, 16, QD), BF),
            pltpu.VMEM((CL * LBL, D), BF),
            pltpu.VMEM((CL * LBL, D), BF),
            pltpu.VMEM((D, CL * LBL), BF),
            pltpu.VMEM((CL * LBL, D), F32),
            pltpu.VMEM((CL, GROUP * 16, D), BF),
            pltpu.VMEM((GROUP * CL, 256), F32),
            pltpu.VMEM((GROUP * CL, 256), F32),
            pltpu.VMEM((GROUP, 8, 128), F32),
            pltpu.VMEM((CL, 8, GROUP * 16), F32),
            pltpu.VMEM((D, D), F32),
            pltpu.VMEM((384, D), F32),
            pltpu.VMEM((3, 3, 96, 256), F32),
            pltpu.VMEM((3, 3, 24, 256), F32),
            pltpu.VMEM((3, 4, 24, 256), F32),
            pltpu.VMEM((3, 96, 256), F32),
            pltpu.VMEM((3, 24, 256), F32),
            pltpu.VMEM((3, 96, 256), F32),
            pltpu.VMEM((D, D), F32),
            pltpu.VMEM((CL * LBL, D), BF),
            dma, dma,
            dma((3, 12, 2)), dma((3, 12, 2)),
            dma((3, 3, 3)), dma((3, 3, 3)),
            dma((3, 4, 4)), dma((3, 4, 4)),
            dma((3, 4)), dma((3, 4)),
            dma((47,)), dma((47,)),
        ],
        compiler_params=pltpu.CompilerParams(
            collective_id=0, has_side_effects=True, vmem_limit_bytes=63 * 1024 * 1024
        ),
        cost_estimate=pl.CostEstimate(flops=20 * 10**9, bytes_accessed=20 * 10**6, transcendentals=0),
    )(queries, meta, projection, tri, accumulator.reshape(16, 128), labels)
    return new_labels, sums.reshape(-1), proj.T


def solution(mesh):
    in_specs = (
        P(("group", "shard"), None),
        P(),
        P(("group", "shard"), None),
        P(("group", "shard")),
        P(("group", "shard"), None),
        P(("group", "shard"), None),
    )
    out_specs = (P(("group", "shard"), None), P(("group", "shard")), P())
    return jax.shard_map(
        on_device, mesh=mesh, in_specs=in_specs, out_specs=out_specs, check_vma=False
    )
```

time: 670 us -> 168 us (0.25); the launches traced: 660 us -> 167 us
  waiting for transfers between devices: 440 us -> 0 us
  Pallas kernels: 0 us -> 158 us
  matrix products: 77.8 us -> 0 us
  local copies, waits for them, and re-layouts: 56.4 us -> 5.55 us
  starting transfers between devices: 44.7 us -> 0 us
  other arithmetic: 26.3 us -> 2.88 us
  between operations: 15.3 us -> 0.66 us
    all_to_all x3 -> x0, waiting for transfers between devices: 291 us -> none  [the longest x1 145 us: bring_back(): lax.all_to_all(query_grad.reshape(1, local_clusters, groups * shards * ca...]
    pallas_call x0 -> x1, Pallas kernels: none -> 158 us  [on_device(): pl.pallas_call(kernel, out_shape=(jax.ShapeDtypeStruct((CL * LBL, D), BF)...]
    psum x1 -> x0, waiting for transfers between devices: 149 us -> none  [on_device(): summed_grad = lax.psum(partial_grad, ('group', 'shard'))]
    dot_general x10 -> x0, matrix products: 77.8 us -> none  [the longest x1 13 us: owner_update(): jnp.einsum('csl,csd->cld', signal, row_vectors, preferred_element_type=jn...]
    all_to_all x3 -> x0, starting transfers between devices: 44.6 us -> none  [the longest x1 19.9 us: deliver(): lax.all_to_all(payload, ('group', 'shard'), split_axis=0, concat_axis=2,...]
    reshape x5 -> x0, local copies, waits for them, and re-layouts: 27.3 us -> none  [the longest x1 14.2 us: bring_back(): query_grad.reshape(1, local_clusters, groups * shards * capacity, features)]
    all_to_all x2 -> x0, local copies, waits for them, and re-layouts: 13.8 us -> none  [bring_back(): lax.all_to_all(query_grad.reshape(1, local_clusters, groups * shards * ca...]
    convert_element_type x4 -> x0, local copies, waits for them, and re-layouts: 9.76 us -> none  [the longest x2 6.14 us: owner_update(): target_marks.astype(jnp.float32)[..., None] == label_index]
  transfers between devices with their start and end apart: 4 -> 0, of which waited for: 3 -> 0; matrix products, arithmetic and copies ran while one was open for 11% -> 0% of each run, Pallas kernels for 0% -> 0%
where the time goes in v1:
time: 168 us; the launch traced here: 167 us
  Pallas kernels  158 us (94%)
  local copies, waits for them, and re-layouts  5.55 us (3%)
  other arithmetic  2.88 us (2%)
    pallas_call x1, Pallas kernels, on_device(): pl.pallas_call(kernel, out_shape=(jax.ShapeDtypeStruct((CL * LBL, D), BF)...  158 us
    unnamed x7, local copies, waits for them, and re-layouts  5.47 us

profile of v1, /device:TPU:1, one launch (start us, length us, event | category | flops | bytes accessed | tf_op | source)
XLA Modules:
  0.0 167.3 jit_solution(830429495923355768)
XLA Ops:
  0.6 0.1 pad.2.clone
  0.7 0.7 fusion.11
  1.4 0.7 fusion.9
  2.2 0.7 maximum_maximum_fusion
  2.9 0.8 fusion.1.tri_ref
  3.6 158.2 %shard_map.85 = (bf16[2048,768]{1,0:T(8,128)(2,1)}, f32[16,128]{1,0:T(8,128)}, f32[768,768]{1,0:T(8,128)}) custom-call(bf16[128,768]{1,0:T(8,128)(2,1)} %q_ref.1, bf16[3,16,128]{2,1,0:T(8,128)(2,1)} %bitcast.9, bf16[768,768]{1,0:T(8,128)(2,1)} %p_ref.1, bf16[256,256]{1,0:T(8,128)(2,1)} %fusion.1.tri_ref, f32[16,128]{1,0:T(8,128)} %bitcast.11, ...), custom_call_target="tpu_custom_call" | custom-call | flops 20000000000 | bytes 20000000 | tf_op jit(solution)/shard_map/pallas_call | solution.py:479
  161.8 0.0 copy-start
  161.8 3.2 %copy.9 = f32[768,768]{1,0:T(8,128)} copy(f32[768,768]{0,1:T(8,128)} %bitcast.8) | data formatting | bytes 4718592
  165.0 0.0 copy-done
  165.0 0.0 copy-start.1
  165.0 1.7 copy.12
  166.7 0.0 copy-done.1
  166.7 0.6 copy.13
  (3 shorter events, 0.0 us)
Async XLA Ops:
  161.8 3.2 %copy-start = (bf16[2048,768]{1,0:T(8,128)(2,1)S(1)}, bf16[2048,768]{1,0:T(8,128)(2,1)}, u32[]{:S(2)}) copy-start(bf16[2048,768]{1,0:T(8,128)(2,1)} %get-tuple-element.17) | copy-start | bytes 9437188
  165.0 1.7 copy-start.1

commit v2 on v1

v2 whole, which is shorter than its diff:
```python
import functools
import math

import jax
import jax.numpy as jnp
from jax import lax
from jax.experimental import pallas as pl
from jax.experimental.pallas import tpu as pltpu
from jax.sharding import PartitionSpec as P

MESH = pl.DeviceIdType.MESH
LBL = 256
QD = 128
D = 768
CL = 8
W = 8
BF = jnp.bfloat16
F32 = jnp.float32
ORDERS = ((0, 1, 2), (1, 2, 0), (2, 0, 1))
PLACE = {1: 1, 2: 3, 3: 2}
GROUP = 16
GROUPS = 4


def arrival(place):
    worst = 0
    for order in ORDERS:
        third, second = place[order[2]], place[order[1]]
        if third == 0:
            tick = (0, 1, 1, 2)[second]
        else:
            tick = (3 + second) if third in (1, 2) else 4 + second
        worst = max(worst, tick)
    return worst


CHIPS = sorted(
    [(a, b, c) for a in range(4) for b in range(4) for c in range(4)],
    key=lambda o: (arrival(o), o),
)


def dot(a, b, ca=1, cb=0):
    return lax.dot_general(a, b, (((ca,), (cb,)), ((), ())), preferred_element_type=F32)


def split(value):
    high = value.astype(BF)
    return high, (value - high.astype(F32)).astype(BF)


def kernel(
    q_ref, meta_ref, p_ref, acc_ref, l_hbm,
    new_hbm, sums_ref, proj_ref, factor_ref,
    gq, gm, lab, lp, lt, total, rows, cp, cd, oh, mk, mc, pj, rb0, sb, rb1, rb2, rb3, s1, s2, g1, g1b, full,
    sem_l, sem_o,
    qs, qr, ms, mr, bs, br, bms, bmr, rs, rr,
):
    y = lax.axis_index("group")
    s = lax.axis_index("shard")
    x, z, k = s // 8, (s // 2) % 4, s % 2
    here = (x, y, z)
    at = [[here[a] for a in order] for order in ORDERS]
    scale = 1.0 / math.sqrt(D)
    T3 = range(3)

    def device(c, core):
        return (c[1], (c[0] * 4 + c[2]) * 2 + core)

    def shifted(axis, r):
        c = list(here)
        c[axis] = (c[axis] + r) % 4
        return device(c, k)

    sibling = device(here, 1 - k)
    partner = [[shifted(axis, r) for r in (1, 2, 3)] for axis in range(3)]

    pending = []

    def remote(src, dst, ssem, rsem, target):
        pltpu.make_async_remote_copy(
            src_ref=src, dst_ref=dst, send_sem=ssem, recv_sem=rsem,
            device_id=target, device_id_type=MESH,
        ).start()
        pending.append((src, ssem))

    def arrived(dst, rsem):
        pltpu.make_async_remote_copy(
            src_ref=dst, dst_ref=dst, send_sem=rsem, recv_sem=rsem,
            device_id=sibling, device_id_type=MESH,
        ).wait_recv()

    barrier = pltpu.get_barrier_semaphore()
    for axis in range(3):
        for r in range(3):
            pl.semaphore_signal(barrier, inc=1, device_id=partner[axis][r], device_id_type=MESH)
    pl.semaphore_signal(barrier, inc=1, device_id=sibling, device_id_type=MESH)
    load = pltpu.make_async_copy(l_hbm, lab, sem_l)
    load.start()

    turned_meta = meta_ref[...].T
    for t in T3:
        gm[t, k, 0, 0, 0] = turned_meta[t * 16:(t + 1) * 16, :].astype(BF)
        gq[t, k, 0, 0, 0] = q_ref[:, t * 256:(t + 1) * 256]
    total[...] = jnp.zeros_like(total)
    pl.semaphore_wait(barrier, 10)

    UNITS = ((0, 0, (0, 1)), (1, 0, (0, 1)), (1, 0, (1, 3)), (2, 0, (0, 1)), (2, 0, (1, 3)), (2, 1, (0, 4)), (2, 2, (0, 4)), (2, 3, (0, 4)))

    def region(t, n, place):
        ring, j, (lo, size) = UNITS[n]
        if ring == 0:
            return gq.at[t, k, 0, 0, pl.ds(place, 1)]
        if ring == 1:
            return gq.at[t, k, 0, place, pl.ds(lo, size)]
        return gq.at[t, k, place, j, pl.ds(lo, size)]

    def half(ref, way):
        return ref.at[:, pl.ds(64 * way, 64)]

    def toward(t, n, way):
        return partner[ORDERS[t][UNITS[n][0]]][0 if way == 0 else 2]

    def both_ways(t, n):
        for way in (0, 1):
            remote(region(t, n, 0), region(t, n, 1 + way), qs.at[t, n, 0, way], qr.at[t, n, 0, way], toward(t, n, way))

    def onward(t, n, way):
        arrived(region(t, n, 1 + way), qr.at[t, n, 0, way])
        remote(
            half(region(t, n, 1 + way), way), half(region(t, n, 3), way),
            qs.at[t, n, 1, way], qr.at[t, n, 1, way], toward(t, n, way),
        )

    def far(t, n):
        for way in (0, 1):
            arrived(half(region(t, n, 3), way), qr.at[t, n, 1, way])

    def meta_region(t, ring, place):
        if ring == 0:
            return gm.at[t, k, 0, 0, place]
        if ring == 1:
            return gm.at[t, k, 0, place]
        return gm.at[t, k, place]

    def meta_send(ring):
        for t in T3:
            for r in (1, 2, 3):
                remote(
                    meta_region(t, ring, 0), meta_region(t, ring, PLACE[r]),
                    ms.at[t, ring, r - 1], mr.at[t, ring, r - 1], partner[ORDERS[t][ring]][r - 1],
                )

    def meta_wait(ring):
        for t in T3:
            for r in (1, 2, 3):
                arrived(meta_region(t, ring, PLACE[r]), mr.at[t, ring, r - 1])

    def to_sibling(t, r3, j):
        ref = gq.at[t, k, r3, j]
        remote(ref, ref, bs.at[t, r3, j], br.at[t, r3, j], sibling)

    def from_sibling(r3s, js):
        for t in T3:
            for r3 in r3s:
                for j in js:
                    arrived(gq.at[t, 1 - k, r3, j], br.at[t, r3, j])

    def meta_sibling(r3):
        for t in T3:
            ref = gm.at[t, k, r3]
            remote(ref, ref, bms.at[t, r3], bmr.at[t, r3], sibling)

    def prepare(c, _):
        here_l = pl.ds(pl.multiple_of(c * LBL, LBL), LBL)
        slab = lab[here_l, :]
        lp[here_l, :] = dot(slab, p_ref[...], 1, 1).astype(BF)
        lt[:, here_l] = slab.T
        return 0

    def prepare_some(lo, hi):
        lax.fori_loop(lo, hi, prepare, 0)

    number = y * 32 + s
    first = number * CL
    octave = first // 128
    base = (128 + first % 128).astype(F32)
    power = lax.shift_left(jnp.int32(1), octave.astype(jnp.int32)).astype(F32)

    def four_chips(group, step):
        words = []
        for h in range(4):
            word = 0
            for n in range(4):
                o = CHIPS[group * GROUP + h * 4 + n]
                word |= (o[0] + 4 * o[1] + 16 * o[2]) << (6 * n)
            words.append(word)
        word = jnp.where(step == 0, words[0], jnp.where(step == 1, words[1], jnp.where(step == 2, words[2], words[3])))
        places = []
        for n in range(4):
            code = (word // (1 << (6 * n))) % 64
            places.append((code % 4, (code // 4) % 4, code // 16))
        return places

    def pair(ref, c, t):
        a1, a2, a3 = ORDERS[t]
        return ref[t, 0, c[a3], c[a2], c[a1]], ref[t, 1, c[a3], c[a2], c[a1]]

    lane = lax.broadcasted_iota(jnp.int32, (16, 256), 1)
    sub = lax.broadcasted_iota(jnp.int32, (16, 256), 0)
    own_slot = jnp.where(sub // W == lane // QD, sub % W, -2).astype(F32)
    own_cluster = (
        lax.broadcasted_iota(jnp.int32, (CL, 128), 0) == lax.broadcasted_iota(jnp.int32, (CL, 128), 1) // 16
    )
    lane_chip = lax.broadcasted_iota(jnp.int32, (8, 128), 1) // 16
    before = lax.broadcasted_iota(jnp.int32, (256, 256), 0)
    after = lax.broadcasted_iota(jnp.int32, (256, 256), 1)
    tri = jnp.where((before < after) & (before // QD == after // QD), 1.0, 0.0).astype(BF)

    def pick(group):
        def names(step, _):
            for u, c in enumerate(four_chips(group, step)):
                a0, a1 = pair(gm, c, 0)
                b0, b1 = pair(gm, c, 1)
                ids = jnp.concatenate(
                    [jnp.concatenate([a0, b0], axis=0), jnp.concatenate([a1, b1], axis=0)], axis=1
                ).astype(F32)
                column = lax.broadcasted_iota(jnp.int32, (32, 256), 0).astype(F32) + 1.0
                found = []
                for n in range(CL):
                    found.append(jnp.sum(jnp.where(ids == (base + n) * power, column, 0.0), axis=0, keepdims=True))
                cp[pl.ds(pl.multiple_of(step * 4 * CL + u * CL, CL), CL), :] = jnp.concatenate(found, axis=0)
            return 0

        lax.fori_loop(0, GROUP // 4, names, 0)
        picked = cp[...] > 0.0
        rank = dot(jnp.where(picked, 1.0, 0.0).astype(BF), tri)
        cd[...] = jnp.where(picked, rank, -1.0)

        def hot(step, _):
            for u, c in enumerate(four_chips(group, step)):
                here_c = pl.ds(pl.multiple_of(step * 4 * CL + u * CL, CL), CL)
                code = cd[here_c, :]
                onehot = jnp.concatenate(
                    [jnp.where(code[n:n + 1, :] == own_slot, 1.0, 0.0).astype(BF) for n in range(CL)], axis=0
                )
                oh[group * GROUP + step * 4 + u] = onehot
                m0, m1 = pair(gm, c, 2)
                marks = jnp.concatenate([m0, m1], axis=1).astype(F32)
                column = cp[here_c, :]
                shifted_marks = jnp.concatenate(
                    [jnp.where(marks[n:n + 1, :] == column, marks[4 + n:5 + n, :], 0.0) for n in range(4)], axis=0
                ).astype(BF)
                spread = dot(shifted_marks, onehot, 1, 1)
                mk[step * 4 + u] = jnp.concatenate(
                    [
                        jnp.sum(jnp.where(own_cluster, spread[n * CL:(n + 1) * CL, :], 0.0), axis=0, keepdims=True)
                        for n in range(4)
                    ]
                    + [jnp.zeros((4, 128), F32)],
                    axis=0,
                )
            return 0

        lax.fori_loop(0, GROUP // 4, hot, 0)
        for h in range(GROUP // 8):
            for n in range(CL):
                line_marks = jnp.zeros((8, 128), F32)
                for i in range(8):
                    turned = pltpu.roll(mk[h * 8 + i], (16 * (i - n)) % 128, 1)
                    line_marks = jnp.where(lane_chip == i, turned, line_marks)
                mc[group, n, :, h * 128:(h + 1) * 128] = line_marks

    def gather_rows(group):
        def choose(step, _):
            for u, c in enumerate(four_chips(group, step)):
                onehot = oh[group * GROUP + step * 4 + u]
                at_row = pl.ds(pl.multiple_of(step * 64 + u * 16, 16), 16)
                for t in T3:
                    q0, q1 = pair(gq, c, t)
                    got = dot(onehot, jnp.concatenate([q0, q1], axis=0)).astype(BF)
                    for n in range(CL):
                        rows[n, at_row, t * 256:(t + 1) * 256] = got[n * 16:(n + 1) * 16, :]
            return 0

        lax.fori_loop(0, GROUP // 4, choose, 0)

    def sum_rows(group):
        def cluster(m0, _):
            ns = [2 * m0, 2 * m0 + 1]
            label = lax.broadcasted_iota(jnp.int32, (LBL, GROUP * 16), 0).astype(F32) + 1.0
            places = [pl.ds(pl.multiple_of(n * LBL, LBL), LBL) for n in ns]
            scores = [dot(lp[h, :], rows[n], 1, 1) * scale for n, h in zip(ns, places)]
            signals = []
            for n, score in zip(ns, scores):
                m = mc[group, n]
                hit = (m[0:1] == label) | (m[1:2] == label) | (m[2:3] == label) | (m[3:4] == label)
                signals.append((1.0 / (1.0 + jnp.exp(-score)) - jnp.where(hit, 1.0, 0.0)).astype(BF))
            for n, h, signal in zip(ns, places, signals):
                total[h, :] += dot(signal, rows[n])
            return 0

        lax.fori_loop(0, CL // 2, cluster, 0)

    def group_work(group):
        gather_rows(group)
        sum_rows(group)

    for t in T3:
        both_ways(t, 0)
    meta_send(0)
    for t in T3:
        both_ways(t, 1)
        both_ways(t, 3)
    for t in T3:
        for way in (0, 1):
            onward(t, 0, way)
    meta_wait(0)
    meta_send(1)
    for t in T3:
        far(t, 0)
        both_ways(t, 2)
        both_ways(t, 4)
        to_sibling(t, 0, 0)
    for t in T3:
        for way in (0, 1):
            onward(t, 1, way)
            onward(t, 3, way)
    load.wait()
    prepare_some(0, 1)
    meta_wait(1)
    meta_send(2)
    meta_sibling(0)
    prepare_some(1, 3)
    for way in (0, 1):
        for t in T3:
            onward(t, 2, way)
            both_ways(t, 5 + way)
            to_sibling(t, 0, 1 + way)
    meta_wait(2)
    for r3 in (1, 2, 3):
        meta_sibling(r3)
    prepare_some(3, 8)
    for t in T3:
        far(t, 1)
        far(t, 2)
        both_ways(t, 7)
        to_sibling(t, 0, 3)
    for t in T3:
        for way in (0, 1):
            onward(t, 4, way)
            to_sibling(t, 1 + way, 0)
    for t in T3:
        for r3 in range(4):
            arrived(gm.at[t, 1 - k, r3], bmr.at[t, r3])
    pick(0)
    pick(1)

    def lines_after(j):
        for t in T3:
            for way in (0, 1):
                onward(t, 4 + j, way)
                to_sibling(t, 1 + way, j)

    def far_after(ns, j):
        for t in T3:
            for n in ns:
                far(t, n)
            to_sibling(t, 3, j)

    lines_after(1)
    pick(2)
    far_after((3, 4), 0)
    pick(3)
    lines_after(2)
    from_sibling((0,), range(4))
    from_sibling((1, 2), (0, 1))
    from_sibling((3,), (0,))
    group_work(0)
    far_after((5,), 1)
    lines_after(3)
    from_sibling((1, 2), (2,))
    from_sibling((3,), (1,))
    group_work(1)
    far_after((6,), 2)
    from_sibling((1, 2), (3,))
    from_sibling((3,), (2,))
    group_work(2)
    far_after((7,), 3)
    from_sibling((3,), (3,))
    group_work(3)

    def halve(n, _):
        rows[n] = total[pl.ds(pl.multiple_of(n * LBL, LBL), LBL), :].astype(BF)
        return 0

    lax.fori_loop(0, CL, halve, 0)

    def project(which):
        at_half = pl.ds(pl.multiple_of(which * 384, 128), 384)
        for t in T3:
            for m in range(2):
                add = dot(lt[at_half, m * 1024:(m + 1) * 1024], rows[m * 4:(m + 1) * 4, :, t * 256:(t + 1) * 256].reshape(1024, 256))
                if m == 0:
                    pj[at_half, t * 256:(t + 1) * 256] = add
                else:
                    pj[at_half, t * 256:(t + 1) * 256] += add

    other_half = pl.ds(pl.multiple_of((1 - k) * 384, 128), 384)
    own_half = pl.ds(pl.multiple_of(k * 384, 128), 384)
    project(1 - k)
    remote(pj.at[other_half], rb0, rs.at[0], rr.at[0], sibling)
    project(k)

    eye = lax.broadcasted_iota(jnp.int32, (128, 128), 0) == lax.broadcasted_iota(jnp.int32, (128, 128), 1)

    def adagrad(n, _):
        here_l = pl.ds(pl.multiple_of(n * LBL, LBL), LBL)
        high, low = split(total[here_l, :])
        grad = (dot(high, p_ref[...]) + dot(low, p_ref[...])) * scale
        mean = jnp.sum(grad * grad, axis=1, keepdims=True) * (1.0 / D)
        old = jnp.concatenate(
            [
                jnp.sum(jnp.where(eye, acc_ref[pl.ds(n * 2 + h, 1), :], 0.0), axis=1, keepdims=True)
                for h in range(2)
            ],
            axis=0,
        )
        sums = old + mean
        for h in range(2):
            sums_ref[pl.ds(n * 2 + h, 1), :] = jnp.sum(
                jnp.where(eye, sums[h * 128:(h + 1) * 128], 0.0), axis=0, keepdims=True
            )
        rows[n] = (lab[here_l, :].astype(F32) - grad * (1.0 / jnp.sqrt(sums))).astype(BF)
        return 0

    def adagrad_some(lo, hi):
        lax.fori_loop(lo, hi, adagrad, 0)

    arrived(rb0, rr.at[0])
    mine_sum = pj[own_half, :] + rb0[...]
    sb[...] = mine_sum.astype(BF)

    def cols(t):
        return pl.ds(t * 256, 256)

    def exchange(n, t, ring, src_of, dst_of):
        for r in (1, 2, 3):
            slot = 1 + n * 9 + t * 3 + r - 1
            remote(src_of(r), dst_of(r), rs.at[slot], rr.at[slot], partner[ORDERS[t][ring]][r - 1])

    def exchanged(n, t, ring, dst_of):
        for r in (1, 2, 3):
            slot = 1 + n * 9 + t * 3 + r - 1
            arrived(dst_of(r, (at[t][ring] - r + 4) % 4), rr.at[slot])

    def piece(i):
        return pl.ds(pl.multiple_of(i * 96, 32), 96)

    def full_piece(i):
        return pl.ds(pl.multiple_of(k * 384 + i * 96, 32), 96)

    def quarter(i):
        return pl.ds(pl.multiple_of(i * 24, 8), 24)

    for t in T3:
        exchange(0, t, 0, lambda r: sb.at[piece((at[t][0] + r) % 4), cols(t)], lambda r: rb1.at[t, r - 1])
    adagrad_some(0, 2)
    for t in T3:
        exchanged(0, t, 0, lambda r, i: rb1.at[t, r - 1])
        s1[t] = (
            (sb[piece(at[t][0]), cols(t)].astype(F32) + rb1[t, 0].astype(F32))
            + (rb1[t, 1].astype(F32) + rb1[t, 2].astype(F32))
        )
        exchange(1, t, 1, lambda r: s1.at[t, quarter((at[t][1] + r) % 4)], lambda r: rb2.at[t, r - 1])
    adagrad_some(2, 3)
    for t in T3:
        exchanged(1, t, 1, lambda r, i: rb2.at[t, r - 1])
        s2[t] = s1[t, quarter(at[t][1])] + rb2[t, 0] + rb2[t, 1] + rb2[t, 2]
        rb3[t, at[t][2]] = s2[t]
        exchange(2, t, 2, lambda r: s2.at[t], lambda r: rb3.at[t, at[t][2]])
    adagrad_some(3, 4)
    for t in T3:
        exchanged(2, t, 2, lambda r, i: rb3.at[t, i])
        mine = quarter(at[t][1])
        g1[t, mine] = (rb3[t, 0] + rb3[t, 1]) + (rb3[t, 2] + rb3[t, 3])
        exchange(3, t, 1, lambda r: g1.at[t, mine], lambda r: g1.at[t, mine])
    adagrad_some(4, 5)
    for t in T3:
        exchanged(3, t, 1, lambda r, i: g1.at[t, quarter(i)])
        g1b[t] = g1[t].astype(BF)
        full[full_piece(at[t][0]), cols(t)] = g1b[t]
        exchange(4, t, 0, lambda r: g1b.at[t], lambda r: full.at[full_piece(at[t][0]), cols(t)])
    adagrad_some(5, 7)
    for t in T3:
        exchanged(4, t, 0, lambda r, i: full.at[full_piece(i), cols(t)])
    remote(full.at[own_half], full.at[own_half], rs.at[46], rr.at[46], sibling)
    adagrad_some(7, 8)
    store = pltpu.make_async_copy(rows, new_hbm, sem_o)
    store.start()
    arrived(full.at[other_half], rr.at[46])

    proj_ref[...] = full[...]
    wide = full[...].astype(F32)
    squares = jnp.sum(wide * wide) * (scale * scale)
    factor = jnp.minimum(1.0, D / jnp.sqrt(squares + 1e-06)) * scale
    factor_ref[...] = jnp.full((8, 128), 1.0, F32) * factor

    store.wait()
    for src, ssem in pending:
        pltpu.make_async_remote_copy(
            src_ref=src, dst_ref=src, send_sem=ssem, recv_sem=ssem,
            device_id=sibling, device_id_type=MESH,
        ).wait_send()


def on_device(queries, projection, labels, accumulator, shortlist, positives):
    ids = shortlist.astype(jnp.int32)
    codes = lax.shift_left(128 + (ids & 127), lax.shift_right_logical(ids, 7))
    marks = jnp.concatenate([lax.shift_right_logical(positives, 8) + 1, (positives & 255) + 1], axis=1)
    meta = jnp.concatenate([codes, marks, jnp.zeros((QD, 88), jnp.int32)], axis=1).astype(F32)
    vmem = pl.BlockSpec(memory_space=pltpu.VMEM)
    hbm = pl.BlockSpec(memory_space=pl.ANY)
    dma = pltpu.SemaphoreType.DMA
    new_labels, sums, proj, factor = pl.pallas_call(
        kernel,
        out_shape=(
            jax.ShapeDtypeStruct((CL, LBL, D), BF),
            jax.ShapeDtypeStruct((16, 128), F32),
            jax.ShapeDtypeStruct((D, D), BF),
            jax.ShapeDtypeStruct((8, 128), F32),
        ),
        in_specs=[vmem] * 4 + [hbm],
        out_specs=(hbm, vmem, vmem, vmem),
        scratch_shapes=[
            pltpu.VMEM((3, 2, 4, 4, 4, QD, 256), BF),
            pltpu.VMEM((3, 2, 4, 4, 4, 16, QD), BF),
            pltpu.VMEM((CL * LBL, D), BF),
            pltpu.VMEM((CL * LBL, D), BF),
            pltpu.VMEM((D, CL * LBL), BF),
            pltpu.VMEM((CL * LBL, D), F32),
            pltpu.VMEM((CL, GROUP * 16, D), BF),
            pltpu.VMEM((GROUP * CL, 256), F32),
            pltpu.VMEM((GROUP * CL, 256), F32),
            pltpu.VMEM((64, 128, 256), BF),
            pltpu.VMEM((GROUP, 8, 128), F32),
            pltpu.VMEM((GROUPS, CL, 8, GROUP * 16), F32),
            pltpu.VMEM((D, D), F32),
            pltpu.VMEM((384, D), F32),
            pltpu.VMEM((384, D), BF),
            pltpu.VMEM((3, 3, 96, 256), BF),
            pltpu.VMEM((3, 3, 24, 256), F32),
            pltpu.VMEM((3, 4, 24, 256), F32),
            pltpu.VMEM((3, 96, 256), F32),
            pltpu.VMEM((3, 24, 256), F32),
            pltpu.VMEM((3, 96, 256), F32),
            pltpu.VMEM((3, 96, 256), BF),
            pltpu.VMEM((D, D), BF),
            dma, dma,
            dma((3, 8, 2, 2)), dma((3, 8, 2, 2)),
            dma((3, 3, 3)), dma((3, 3, 3)),
            dma((3, 4, 4)), dma((3, 4, 4)),
            dma((3, 4)), dma((3, 4)),
            dma((47,)), dma((47,)),
        ],
        compiler_params=pltpu.CompilerParams(
            collective_id=0, has_side_effects=True, vmem_limit_bytes=63 * 1024 * 1024
        ),
        cost_estimate=pl.CostEstimate(flops=20 * 10**9, bytes_accessed=20 * 10**6, transcendentals=0),
    )(queries, meta, projection, accumulator.reshape(16, 128), labels)
    proj_grad = proj.T.astype(F32) * factor[0, 0]
    return new_labels.reshape(CL * LBL, D), sums.reshape(-1), proj_grad


def solution(mesh):
    in_specs = (
        P(("group", "shard"), None),
        P(),
        P(("group", "shard"), None),
        P(("group", "shard")),
        P(("group", "shard"), None),
        P(("group", "shard"), None),
    )
    out_specs = (P(("group", "shard"), None), P(("group", "shard")), P())
    return jax.shard_map(
        on_device, mesh=mesh, in_specs=in_specs, out_specs=out_specs, check_vma=False
    )
```

time: 168 us -> 130 us (0.77)
  Pallas kernels: 158 us -> 117 us
  local copies, waits for them, and re-layouts: 5.55 us -> 9.19 us
    pallas_call x1, Pallas kernels: 158 us -> 117 us  [on_device(): pl.pallas_call(kernel, out_shape=(jax.ShapeDtypeStruct((CL, LBL, D), BF),...]
    unnamed x7, local copies, waits for them, and re-layouts: 5.47 us -> 7.93 us
    mul x0 -> x1, other arithmetic: none -> 2.07 us  [on_device(): proj_grad = proj.T.astype(F32) * factor[0, 0]]
where the time goes in v2:
time: 130 us; the launch traced here: 129 us
  Pallas kernels  117 us (90%)
  local copies, waits for them, and re-layouts  9.19 us (7%)
  other arithmetic  2.83 us (2%)
    pallas_call x1, Pallas kernels, on_device(): pl.pallas_call(kernel, out_shape=(jax.ShapeDtypeStruct((CL, LBL, D), BF),...  117 us
    unnamed x7, local copies, waits for them, and re-layouts  7.93 us

profile of v2, /device:TPU:1, one launch (start us, length us, event | category | flops | bytes accessed | tf_op | source)
XLA Modules:
  0.0 129.2 jit_solution(15402298202345746440)
XLA Ops:
  0.6 0.1 pad.3.clone
  0.7 0.8 copy.14
  1.5 0.8 copy.17
  2.4 0.7 add_convert_fusion.meta_ref
  3.1 116.5 %shard_map.85 = (bf16[8,256,768]{2,1,0:T(8,128)(2,1)}, f32[16,128]{1,0:T(8,128)}, bf16[768,768]{1,0:T(8,128)(2,1)}, f32[8,128]{1,0:T(8,128)}) custom-call(bf16[128,768]{1,0:T(8,128)(2,1)} %q_ref.1, f32[128,128]{1,0:T(8,128)} %add_convert_fusion.meta_ref, bf16[768,768]{1,0:T(8,128)(2,1)} %p_ref.1, f32[16,128]{1,0:T(8,128)} %bitcast.8, bf16[2048,768]{1,0:T(8,128)(2,1)} %l_hbm.1), custom_call_target="tpu_custom_call" | custom-call | flops 20000000000 | bytes 20000000 | tf_op jit(solution)/shard_map/pallas_call | solution.py:525
  119.6 1.2 slice.3
  120.8 2.1 %multiply_bitcast_fusion = f32[768,768]{0,1:T(8,128)S(1)} fusion(bf16[768,768]{1,0:T(8,128)(2,1)} %get-tuple-element.9, f32[]{:T(128)} %bitcast.3), kind=kLoop, calls=%fused_computation | loop fusion | flops 1179648 | bytes 3538948 | tf_op jit(solution)/shard_map/mul | solution.py:571
  122.9 2.0 %copy.21 = f32[768,768]{1,0:T(8,128)} copy(f32[768,768]{0,1:T(8,128)S(1)} %multiply_bitcast_fusion) | data formatting | bytes 4718592
  124.8 0.0 copy-start
  124.8 3.8 %copy.24 = bf16[2048,768]{1,0:T(8,128)(2,1)} copy(bf16[2048,768]{1,0:T(8,128)(2,1)} %bitcast.6) | data formatting | bytes 6291456
  128.6 0.0 copy-done
  128.6 0.6 copy.25
  (3 shorter events, 0.0 us)
Async XLA Ops:
  124.8 3.8 %copy-start = (f32[16,128]{1,0:T(8,128)S(1)}, f32[16,128]{1,0:T(8,128)}, u32[]{:S(2)}) copy-start(f32[16,128]{1,0:T(8,128)} %get-tuple-element.8) | copy-start | bytes 24580

commit v3 on v2

--- a/solution.py
+++ b/solution.py
@@ -26,10 +26,7 @@
     worst = 0
     for order in ORDERS:
         third, second = place[order[2]], place[order[1]]
-        if third == 0:
-            tick = (0, 1, 1, 2)[second]
-        else:
-            tick = (3 + second) if third in (1, 2) else 4 + second
+        tick = ((0, 0, 0, 0), (1, 2, 4, 6), (1, 2, 4, 6), (3, 5, 7, 8))[third][second]
         worst = max(worst, tick)
     return worst
 
@@ -50,10 +47,10 @@
 
 
 def kernel(
-    q_ref, meta_ref, p_ref, acc_ref, l_hbm,
-    new_hbm, sums_ref, proj_ref, factor_ref,
-    gq, gm, lab, lp, lt, total, rows, cp, cd, oh, mk, mc, pj, rb0, sb, rb1, rb2, rb3, s1, s2, g1, g1b, full,
-    sem_l, sem_o,
+    q_ref, list_ref, pos_ref, p_ref, acc_ref, l_hbm,
+    new_hbm, sums_ref, full_hbm,
+    gq, gm, lab, lp, lt, total, rows, cp, cd, oh, mk, mc, pj, rb0, sb, rb1, rb2, rb3, s1, s2, g1, full,
+    sem_l, sem_o, sem_f,
     qs, qr, ms, mr, bs, br, bms, bmr, rs, rr,
 ):
     y = lax.axis_index("group")
@@ -90,6 +87,14 @@
             device_id=sibling, device_id_type=MESH,
         ).wait_recv()
 
+    def drain():
+        for src, ssem in pending:
+            pltpu.make_async_remote_copy(
+                src_ref=src, dst_ref=src, send_sem=ssem, recv_sem=ssem,
+                device_id=sibling, device_id_type=MESH,
+            ).wait_send()
+        pending.clear()
+
     barrier = pltpu.get_barrier_semaphore()
     for axis in range(3):
         for r in range(3):
@@ -98,14 +103,31 @@
     load = pltpu.make_async_copy(l_hbm, lab, sem_l)
     load.start()
 
-    turned_meta = meta_ref[...].T
-    for t in T3:
-        gm[t, k, 0, 0, 0] = turned_meta[t * 16:(t + 1) * 16, :].astype(BF)
+    ids = list_ref[...]
+    pos = pos_ref[...]
+
+    codes = lax.shift_left(128 + (ids & 127), lax.shift_right_logical(ids, 7)).astype(F32)
+    marks = jnp.concatenate(
+        [
+            (lax.shift_right_logical(pos, 8) + 1).astype(F32),
+            ((pos & 255) + 1).astype(F32),
+            jnp.zeros((8, QD), F32),
+        ],
+        axis=0,
+    )
+    for t, value in enumerate((codes[:16], codes[16:], marks)):
+        gm[t, k, 0, 0, 0] = value.astype(BF)
+    for t in T3:
         gq[t, k, 0, 0, 0] = q_ref[:, t * 256:(t + 1) * 256]
     total[...] = jnp.zeros_like(total)
     pl.semaphore_wait(barrier, 10)
 
-    UNITS = ((0, 0, (0, 1)), (1, 0, (0, 1)), (1, 0, (1, 3)), (2, 0, (0, 1)), (2, 0, (1, 3)), (2, 1, (0, 4)), (2, 2, (0, 4)), (2, 3, (0, 4)))
+    UNITS = (
+        (0, 0, (0, 1)),
+        (1, 0, (0, 1)), (1, 0, (1, 2)), (1, 0, (3, 1)),
+        (2, 0, (0, 1)), (2, 0, (1, 2)), (2, 0, (3, 1)),
+        (2, 1, (0, 4)), (2, 2, (0, 4)), (2, 3, (0, 4)),
+    )
 
     def region(t, n, place):
         ring, j, (lo, size) = UNITS[n]
@@ -156,15 +178,22 @@
             for r in (1, 2, 3):
                 arrived(meta_region(t, ring, PLACE[r]), mr.at[t, ring, r - 1])
 
+    landed, shared = set(), set()
+
     def to_sibling(t, r3, j):
         ref = gq.at[t, k, r3, j]
         remote(ref, ref, bs.at[t, r3, j], br.at[t, r3, j], sibling)
-
-    def from_sibling(r3s, js):
-        for t in T3:
-            for r3 in r3s:
-                for j in js:
-                    arrived(gq.at[t, 1 - k, r3, j], br.at[t, r3, j])
+        landed.add((t, r3, j))
+
+    def require(group):
+        lines = set()
+        for o in CHIPS[group * GROUP:(group + 1) * GROUP]:
+            for t in T3:
+                lines.add((t, o[ORDERS[t][2]], o[ORDERS[t][1]]))
+        assert lines <= landed
+        for t, r3, j in sorted(lines - shared):
+            arrived(gq.at[t, 1 - k, r3, j], br.at[t, r3, j])
+        shared.update(lines)
 
     def meta_sibling(r3):
         for t in T3:
@@ -287,108 +316,128 @@
 
     def sum_rows(group):
         def cluster(m0, _):
-            ns = [2 * m0, 2 * m0 + 1]
             label = lax.broadcasted_iota(jnp.int32, (LBL, GROUP * 16), 0).astype(F32) + 1.0
-            places = [pl.ds(pl.multiple_of(n * LBL, LBL), LBL) for n in ns]
-            scores = [dot(lp[h, :], rows[n], 1, 1) * scale for n, h in zip(ns, places)]
-            signals = []
-            for n, score in zip(ns, scores):
-                m = mc[group, n]
+
+            def place(u):
+                return pl.ds(pl.multiple_of((4 * m0 + u) * LBL, LBL), LBL)
+
+            def scored(u):
+                return dot(lp[place(u), :], rows[4 * m0 + u], 1, 1) * scale
+
+            def signal(u, sc):
+                m = mc[group, 4 * m0 + u]
                 hit = (m[0:1] == label) | (m[1:2] == label) | (m[2:3] == label) | (m[3:4] == label)
-                signals.append((1.0 / (1.0 + jnp.exp(-score)) - jnp.where(hit, 1.0, 0.0)).astype(BF))
-            for n, h, signal in zip(ns, places, signals):
-                total[h, :] += dot(signal, rows[n])
+                return (1.0 / (1.0 + jnp.exp(-sc)) - jnp.where(hit, 1.0, 0.0)).astype(BF)
+
+            scores, signals = [scored(0), scored(1)], []
+            for u in range(4):
+                signals.append(signal(u, scores[u]))
+                if u + 2 < 4:
+                    scores.append(scored(u + 2))
+                if u > 0:
+                    total[place(u - 1), :] += dot(signals[u - 1], rows[4 * m0 + u - 1])
+            total[place(3), :] += dot(signals[3], rows[4 * m0 + 3])
             return 0
 
-        lax.fori_loop(0, CL // 2, cluster, 0)
+        lax.fori_loop(0, CL // 4, cluster, 0)
 
     def group_work(group):
         gather_rows(group)
         sum_rows(group)
 
-    for t in T3:
-        both_ways(t, 0)
+    def every(n, act):
+        for t in T3:
+            for way in (0, 1):
+                act(t, n, way)
+
+    def sharing(n, j):
+        for t in T3:
+            for way in (0, 1):
+                onward(t, n, way)
+                to_sibling(t, 1 + way, j)
+
+    def far_after(ns, j, r3=3):
+        for t in T3:
+            for n in ns:
+                far(t, n)
+            to_sibling(t, r3, j)
+
     meta_send(0)
-    for t in T3:
-        both_ways(t, 1)
-        both_ways(t, 3)
+    for n in (0, 1, 4):
+        for t in T3:
+            both_ways(t, n)
+    load.wait()
+    prepare_some(0, 2)
+    meta_wait(0)
+    meta_send(1)
     for t in T3:
         for way in (0, 1):
             onward(t, 0, way)
-    meta_wait(0)
-    meta_send(1)
-    for t in T3:
-        far(t, 0)
         both_ways(t, 2)
-        both_ways(t, 4)
-        to_sibling(t, 0, 0)
-    for t in T3:
-        for way in (0, 1):
-            onward(t, 1, way)
-            onward(t, 3, way)
-    load.wait()
-    prepare_some(0, 1)
+    every(1, onward)
+    every(4, onward)
+    prepare_some(2, 4)
     meta_wait(1)
     meta_send(2)
     meta_sibling(0)
-    prepare_some(1, 3)
-    for way in (0, 1):
-        for t in T3:
-            onward(t, 2, way)
-            both_ways(t, 5 + way)
+    for t in T3:
+        far(t, 0)
+        both_ways(t, 5)
+        both_ways(t, 3)
+        both_ways(t, 6)
+        to_sibling(t, 0, 0)
+    prepare_some(4, 8)
+    every(2, onward)
+    for t in T3:
+        for way in (0, 1):
+            onward(t, 3, way)
             to_sibling(t, 0, 1 + way)
+        both_ways(t, 7)
     meta_wait(2)
     for r3 in (1, 2, 3):
         meta_sibling(r3)
-    prepare_some(3, 8)
-    for t in T3:
-        far(t, 1)
-        far(t, 2)
-        both_ways(t, 7)
-        to_sibling(t, 0, 3)
+    every(5, onward)
     for t in T3:
         for way in (0, 1):
-            onward(t, 4, way)
+            onward(t, 6, way)
             to_sibling(t, 1 + way, 0)
+        both_ways(t, 8)
     for t in T3:
         for r3 in range(4):
             arrived(gm.at[t, 1 - k, r3], bmr.at[t, r3])
     pick(0)
+    far_after((1, 2, 3), 3, 0)
     pick(1)
-
-    def lines_after(j):
-        for t in T3:
-            for way in (0, 1):
-                onward(t, 4 + j, way)
-                to_sibling(t, 1 + way, j)
-
-    def far_after(ns, j):
-        for t in T3:
-            for n in ns:
-                far(t, n)
-            to_sibling(t, 3, j)
-
-    lines_after(1)
+    for t in T3:
+        for way in (0, 1):
+            onward(t, 7, way)
+            to_sibling(t, 1 + way, 1)
+        both_ways(t, 9)
     pick(2)
-    far_after((3, 4), 0)
+    far_after((4, 5, 6), 0)
+    require(0)
+    gather_rows(0)
+    sum_rows(0)
+    sharing(8, 2)
     pick(3)
-    lines_after(2)
-    from_sibling((0,), range(4))
-    from_sibling((1, 2), (0, 1))
-    from_sibling((3,), (0,))
-    group_work(0)
-    far_after((5,), 1)
-    lines_after(3)
-    from_sibling((1, 2), (2,))
-    from_sibling((3,), (1,))
-    group_work(1)
-    far_after((6,), 2)
-    from_sibling((1, 2), (3,))
-    from_sibling((3,), (2,))
-    group_work(2)
-    far_after((7,), 3)
-    from_sibling((3,), (3,))
-    group_work(3)
+    far_after((7,), 1)
+    require(1)
+    gather_rows(1)
+    sum_rows(1)
+    sharing(9, 3)
+    far_after((8,), 2)
+    require(2)
+    gather_rows(2)
+    far_after((9,), 3)
+    sum_rows(2)
+    require(3)
+    gather_rows(3)
+    sum_rows(3)
+    for t in T3:
+        for r3 in range(4):
+            for j in range(4):
+                if (t, r3, j) not in shared:
+                    arrived(gq.at[t, 1 - k, r3, j], br.at[t, r3, j])
 
     def halve(n, _):
         rows[n] = total[pl.ds(pl.multiple_of(n * LBL, LBL), LBL), :].astype(BF)
@@ -432,6 +481,7 @@
                 jnp.where(eye, sums[h * 128:(h + 1) * 128], 0.0), axis=0, keepdims=True
             )
         rows[n] = (lab[here_l, :].astype(F32) - grad * (1.0 / jnp.sqrt(sums))).astype(BF)
+        pltpu.make_async_copy(rows.at[n], new_hbm.at[here_l], sem_o.at[n]).start()
         return 0
 
     def adagrad_some(lo, hi):
@@ -460,78 +510,119 @@
     def full_piece(i):
         return pl.ds(pl.multiple_of(k * 384 + i * 96, 32), 96)
 
-    def quarter(i):
-        return pl.ds(pl.multiple_of(i * 24, 8), 24)
+    def tiles(i):
+        return pl.ds(i * 3, 3)
+
+    def laid(r, l):
+        return r * 2 + l, slice(r * 16, (r + 1) * 16), slice(l * 128, (l + 1) * 128)
+
+    TILES = [laid(r, l) for r in range(6) for l in range(2)]
 
     for t in T3:
         exchange(0, t, 0, lambda r: sb.at[piece((at[t][0] + r) % 4), cols(t)], lambda r: rb1.at[t, r - 1])
     adagrad_some(0, 2)
+    drain()
     for t in T3:
         exchanged(0, t, 0, lambda r, i: rb1.at[t, r - 1])
-        s1[t] = (
+        summed = (
             (sb[piece(at[t][0]), cols(t)].astype(F32) + rb1[t, 0].astype(F32))
             + (rb1[t, 1].astype(F32) + rb1[t, 2].astype(F32))
-        )
-        exchange(1, t, 1, lambda r: s1.at[t, quarter((at[t][1] + r) % 4)], lambda r: rb2.at[t, r - 1])
+        ).astype(BF)
+        for n, down, across in TILES:
+            s1[t, n] = summed[down, across]
+        exchange(1, t, 1, lambda r: s1.at[t, tiles((at[t][1] + r) % 4)], lambda r: rb2.at[t, r - 1])
     adagrad_some(2, 3)
     for t in T3:
         exchanged(1, t, 1, lambda r, i: rb2.at[t, r - 1])
-        s2[t] = s1[t, quarter(at[t][1])] + rb2[t, 0] + rb2[t, 1] + rb2[t, 2]
+        s2[t] = (
+            (s1[t, tiles(at[t][1])].astype(F32) + rb2[t, 0].astype(F32))
+            + (rb2[t, 1].astype(F32) + rb2[t, 2].astype(F32))
+        ).astype(BF)
         rb3[t, at[t][2]] = s2[t]
         exchange(2, t, 2, lambda r: s2.at[t], lambda r: rb3.at[t, at[t][2]])
     adagrad_some(3, 4)
     for t in T3:
         exchanged(2, t, 2, lambda r, i: rb3.at[t, i])
-        mine = quarter(at[t][1])
-        g1[t, mine] = (rb3[t, 0] + rb3[t, 1]) + (rb3[t, 2] + rb3[t, 3])
+        mine = tiles(at[t][1])
+        g1[t, mine] = (
+            (rb3[t, 0].astype(F32) + rb3[t, 1].astype(F32)) + (rb3[t, 2].astype(F32) + rb3[t, 3].astype(F32))
+        ).astype(BF)
         exchange(3, t, 1, lambda r: g1.at[t, mine], lambda r: g1.at[t, mine])
     adagrad_some(4, 5)
-    for t in T3:
-        exchanged(3, t, 1, lambda r, i: g1.at[t, quarter(i)])
-        g1b[t] = g1[t].astype(BF)
-        full[full_piece(at[t][0]), cols(t)] = g1b[t]
-        exchange(4, t, 0, lambda r: g1b.at[t], lambda r: full.at[full_piece(at[t][0]), cols(t)])
+
+    def share_piece(t, r):
+        ref = full.at[full_piece((at[t][0] - r + 4) % 4), cols(t)]
+        remote(ref, ref, rs.at[46 + t * 4 + r], rr.at[46 + t * 4 + r], sibling)
+
+    for t in T3:
+        exchanged(3, t, 1, lambda r, i: g1.at[t, tiles(i)])
+        summed = jnp.concatenate(
+            [jnp.concatenate([g1[t, 2 * r], g1[t, 2 * r + 1]], axis=1) for r in range(6)], axis=0
+        )
+        mine = full.at[full_piece(at[t][0]), cols(t)]
+        mine[...] = summed
+        exchange(4, t, 0, lambda r: mine, lambda r: mine)
+        share_piece(t, 0)
     adagrad_some(5, 7)
-    for t in T3:
-        exchanged(4, t, 0, lambda r, i: full.at[full_piece(i), cols(t)])
-    remote(full.at[own_half], full.at[own_half], rs.at[46], rr.at[46], sibling)
+    for r in (1, 3, 2):
+        for t in T3:
+            slot = 1 + 4 * 9 + t * 3 + r - 1
+            arrived(full.at[full_piece((at[t][0] - r + 4) % 4), cols(t)], rr.at[slot])
+            share_piece(t, r)
     adagrad_some(7, 8)
-    store = pltpu.make_async_copy(rows, new_hbm, sem_o)
-    store.start()
-    arrived(full.at[other_half], rr.at[46])
-
-    proj_ref[...] = full[...]
-    wide = full[...].astype(F32)
-    squares = jnp.sum(wide * wide) * (scale * scale)
+    for t in T3:
+        for r in range(4):
+            i = (at[t][0] - r + 4) % 4
+            arrived(full.at[pl.ds(pl.multiple_of((1 - k) * 384 + i * 96, 32), 96), cols(t)], rr.at[46 + t * 4 + r])
+    out = pltpu.make_async_copy(full, full_hbm, sem_f)
+    out.start()
+    for n in range(CL):
+        pltpu.make_async_copy(rows.at[n], new_hbm.at[pl.ds(n * LBL, LBL)], sem_o.at[n]).wait()
+    drain()
+    out.wait()
+
+
+def finish(new_hbm, sums_ref, full_hbm, labels_hbm, acc_ref, grad_hbm, held, full, grad, sem_in, sem_out, sem_f, sem_g):
+    parts = [pl.ds(n * LBL, LBL) for n in range(CL)]
+    bands = [pl.ds(n * 128, 128) for n in range(D // 128)]
+    loads = [pltpu.make_async_copy(full_hbm.at[b], full.at[b], sem_f.at[n]) for n, b in enumerate(bands)]
+    stores = [pltpu.make_async_copy(grad.at[b], grad_hbm.at[b], sem_g.at[n]) for n, b in enumerate(bands)]
+    ins = [pltpu.make_async_copy(new_hbm.at[p], held.at[p], sem_in.at[n]) for n, p in enumerate(parts)]
+    outs = [pltpu.make_async_copy(held.at[p], labels_hbm.at[p], sem_out.at[n]) for n, p in enumerate(parts)]
+    for copy in loads + ins:
+        copy.start()
+    acc_ref[...] = sums_ref[...]
+    scale = 1.0 / math.sqrt(D)
+    squares = jnp.zeros((8, D), F32)
+    for n, b in enumerate(bands):
+        loads[n].wait()
+        wide = full[b, :].astype(F32)
+        squares = squares + jnp.sum((wide * wide).reshape(16, 8, D), axis=0)
+    for n in range(CL):
+        ins[n].wait()
+        outs[n].start()
+    squares = jnp.sum(squares, keepdims=True) * (scale * scale)
     factor = jnp.minimum(1.0, D / jnp.sqrt(squares + 1e-06)) * scale
-    factor_ref[...] = jnp.full((8, 128), 1.0, F32) * factor
-
-    store.wait()
-    for src, ssem in pending:
-        pltpu.make_async_remote_copy(
-            src_ref=src, dst_ref=src, send_sem=ssem, recv_sem=ssem,
-            device_id=sibling, device_id_type=MESH,
-        ).wait_send()
+    for n, b in enumerate(bands):
+        grad[b, :] = full[:, n * 128:(n + 1) * 128].astype(F32).T * factor
+        stores[n].start()
+    for copy in outs + stores:
+        copy.wait()
 
 
 def on_device(queries, projection, labels, accumulator, shortlist, positives):
-    ids = shortlist.astype(jnp.int32)
-    codes = lax.shift_left(128 + (ids & 127), lax.shift_right_logical(ids, 7))
-    marks = jnp.concatenate([lax.shift_right_logical(positives, 8) + 1, (positives & 255) + 1], axis=1)
-    meta = jnp.concatenate([codes, marks, jnp.zeros((QD, 88), jnp.int32)], axis=1).astype(F32)
     vmem = pl.BlockSpec(memory_space=pltpu.VMEM)
     hbm = pl.BlockSpec(memory_space=pl.ANY)
     dma = pltpu.SemaphoreType.DMA
-    new_labels, sums, proj, factor = pl.pallas_call(
+    new_labels, sums, proj = pl.pallas_call(
         kernel,
         out_shape=(
-            jax.ShapeDtypeStruct((CL, LBL, D), BF),
+            jax.ShapeDtypeStruct((CL * LBL, D), BF),
             jax.ShapeDtypeStruct((16, 128), F32),
             jax.ShapeDtypeStruct((D, D), BF),
-            jax.ShapeDtypeStruct((8, 128), F32),
         ),
-        in_specs=[vmem] * 4 + [hbm],
-        out_specs=(hbm, vmem, vmem, vmem),
+        in_specs=[vmem] * 5 + [hbm],
+        out_specs=(hbm, vmem, hbm),
         scratch_shapes=[
             pltpu.VMEM((3, 2, 4, 4, 4, QD, 256), BF),
             pltpu.VMEM((3, 2, 4, 4, 4, 16, QD), BF),
@@ -549,27 +640,42 @@
             pltpu.VMEM((384, D), F32),
             pltpu.VMEM((384, D), BF),
             pltpu.VMEM((3, 3, 96, 256), BF),
-            pltpu.VMEM((3, 3, 24, 256), F32),
-            pltpu.VMEM((3, 4, 24, 256), F32),
-            pltpu.VMEM((3, 96, 256), F32),
-            pltpu.VMEM((3, 24, 256), F32),
-            pltpu.VMEM((3, 96, 256), F32),
-            pltpu.VMEM((3, 96, 256), BF),
+            pltpu.VMEM((3, 3, 3, 16, 128), BF),
+            pltpu.VMEM((3, 4, 3, 16, 128), BF),
+            pltpu.VMEM((3, 12, 16, 128), BF),
+            pltpu.VMEM((3, 3, 16, 128), BF),
+            pltpu.VMEM((3, 12, 16, 128), BF),
             pltpu.VMEM((D, D), BF),
-            dma, dma,
-            dma((3, 8, 2, 2)), dma((3, 8, 2, 2)),
+            dma, dma((CL,)), dma,
+            dma((3, 10, 2, 2)), dma((3, 10, 2, 2)),
             dma((3, 3, 3)), dma((3, 3, 3)),
             dma((3, 4, 4)), dma((3, 4, 4)),
             dma((3, 4)), dma((3, 4)),
-            dma((47,)), dma((47,)),
+            dma((58,)), dma((58,)),
         ],
         compiler_params=pltpu.CompilerParams(
             collective_id=0, has_side_effects=True, vmem_limit_bytes=63 * 1024 * 1024
         ),
         cost_estimate=pl.CostEstimate(flops=20 * 10**9, bytes_accessed=20 * 10**6, transcendentals=0),
-    )(queries, meta, projection, accumulator.reshape(16, 128), labels)
-    proj_grad = proj.T.astype(F32) * factor[0, 0]
-    return new_labels.reshape(CL * LBL, D), sums.reshape(-1), proj_grad
+    )(queries, shortlist.T, positives.T, projection, accumulator.reshape(16, 128), labels)
+    labels_out, sums_out, grad = pl.pallas_call(
+        finish,
+        out_shape=(
+            jax.ShapeDtypeStruct((CL * LBL, D), BF),
+            jax.ShapeDtypeStruct((16, 128), F32),
+            jax.ShapeDtypeStruct((D, D), F32),
+        ),
+        in_specs=[hbm, vmem, hbm],
+        out_specs=(hbm, vmem, hbm),
+        scratch_shapes=[
+            pltpu.VMEM((CL * LBL, D), BF),
+            pltpu.VMEM((D, D), BF),
+            pltpu.VMEM((D, D), F32),
+            dma((CL,)), dma((CL,)), dma((D // 128,)), dma((D // 128,)),
+        ],
+        compiler_params=pltpu.CompilerParams(vmem_limit_bytes=63 * 1024 * 1024),
+    )(new_labels, sums, proj)
+    return labels_out, sums_out.reshape(-1), grad
 
 
 def solution(mesh):

time: 130 us -> 112 us (0.86)
  local copies, waits for them, and re-layouts: 9.19 us -> 0 us
  Pallas kernels: 117 us -> 111 us
  other arithmetic: 2.83 us -> 0 us
    unnamed x7 -> x0, local copies, waits for them, and re-layouts: 7.93 us -> none
    pallas_call x1 -> x2, Pallas kernels: 117 us -> 111 us  [the longest x1 105 us: on_device(): pl.pallas_call(kernel, out_shape=(jax.ShapeDtypeStruct((CL * LBL, D), BF)...]
    mul x1 -> x0, other arithmetic: 2.07 us -> none  [on_device(): proj_grad = proj.T.astype(F32) * factor[0, 0]]
where the time goes in v3:
time: 112 us; the launch traced here: 111 us
  Pallas kernels  111 us (99%)
    pallas_call x1, Pallas kernels, on_device(): pl.pallas_call(kernel, out_shape=(jax.ShapeDtypeStruct((CL * LBL, D), BF)...  105 us
    pallas_call x1, Pallas kernels, on_device(): pl.pallas_call(finish, out_shape=(jax.ShapeDtypeStruct((CL * LBL, D), BF)...  6.01 us

profile of v3, /device:TPU:1, one launch (start us, length us, event | category | flops | bytes accessed | tf_op | source)
XLA Modules:
  0.0 111.4 jit_solution(16191753454250294935)
XLA Ops:
  0.6 104.6 %shard_map.85 = (bf16[2048,768]{1,0:T(8,128)(2,1)}, f32[16,128]{1,0:T(8,128)}, bf16[768,768]{1,0:T(8,128)(2,1)}) custom-call(bf16[128,768]{1,0:T(8,128)(2,1)} %q_ref.1, s32[32,128]{1,0:T(8,128)} %bitcast.4, s32[4,128]{1,0:T(4,128)} %bitcast.7, bf16[768,768]{1,0:T(8,128)(2,1)} %p_ref.1, f32[16,128]{1,0:T(8,128)} %bitcast.5, bf16[2048,768]{1,0:T(8,128)(2,1)} %l_hbm.1), custom_call_target="tpu_custom_call" | custom-call | flops 20000000000 | bytes 20000000 | tf_op jit(solution)/shard_map/pallas_call | solution.py:617
  105.3 6.0 %shard_map.86 = (bf16[2048,768]{1,0:T(8,128)(2,1)}, f32[16,128]{1,0:T(8,128)}, f32[768,768]{1,0:T(8,128)}) custom-call(bf16[2048,768]{1,0:T(8,128)(2,1)} %get-tuple-element.9.new_hbm, f32[16,128]{1,0:T(8,128)} %get-tuple-element.10.sums_ref, bf16[768,768]{1,0:T(8,128)(2,1)} %get-tuple-element.11.full_hbm), custom_call_target="tpu_custom_call" | custom-call | tf_op jit(solution)/shard_map/pallas_call | solution.py:661

commit v4 on v3

--- a/solution.py
+++ b/solution.py
@@ -312,7 +312,7 @@
                         rows[n, at_row, t * 256:(t + 1) * 256] = got[n * 16:(n + 1) * 16, :]
             return 0
 
-        lax.fori_loop(0, GROUP // 4, choose, 0)
+        lax.fori_loop(0, GROUP // 4, choose, 0, unroll=2)
 
     def sum_rows(group):
         def cluster(m0, _):
@@ -328,6 +328,12 @@
                 m = mc[group, 4 * m0 + u]
                 hit = (m[0:1] == label) | (m[1:2] == label) | (m[2:3] == label) | (m[3:4] == label)
                 return (1.0 / (1.0 + jnp.exp(-sc)) - jnp.where(hit, 1.0, 0.0)).astype(BF)
+
+            def add(u):
+                summed = total[place(u), :] + dot(signals[u], rows[4 * m0 + u])
+                total[place(u), :] = summed
+                if group == GROUPS - 1:
+                    rows[4 * m0 + u] = summed.astype(BF)
 
             scores, signals = [scored(0), scored(1)], []
             for u in range(4):
@@ -335,8 +341,8 @@
                 if u + 2 < 4:
                     scores.append(scored(u + 2))
                 if u > 0:
-                    total[place(u - 1), :] += dot(signals[u - 1], rows[4 * m0 + u - 1])
-            total[place(3), :] += dot(signals[3], rows[4 * m0 + 3])
+                    add(u - 1)
+            add(3)
             return 0
 
         lax.fori_loop(0, CL // 4, cluster, 0)
@@ -439,12 +445,6 @@
                 if (t, r3, j) not in shared:
                     arrived(gq.at[t, 1 - k, r3, j], br.at[t, r3, j])
 
-    def halve(n, _):
-        rows[n] = total[pl.ds(pl.multiple_of(n * LBL, LBL), LBL), :].astype(BF)
-        return 0
-
-    lax.fori_loop(0, CL, halve, 0)
-
     def project(which):
         at_half = pl.ds(pl.multiple_of(which * 384, 128), 384)
         for t in T3:
@@ -520,7 +520,7 @@
 
     for t in T3:
         exchange(0, t, 0, lambda r: sb.at[piece((at[t][0] + r) % 4), cols(t)], lambda r: rb1.at[t, r - 1])
-    adagrad_some(0, 2)
+    adagrad_some(0, 1)
     drain()
     for t in T3:
         exchanged(0, t, 0, lambda r, i: rb1.at[t, r - 1])
@@ -531,7 +531,7 @@
         for n, down, across in TILES:
             s1[t, n] = summed[down, across]
         exchange(1, t, 1, lambda r: s1.at[t, tiles((at[t][1] + r) % 4)], lambda r: rb2.at[t, r - 1])
-    adagrad_some(2, 3)
+    adagrad_some(1, 3)
     for t in T3:
         exchanged(1, t, 1, lambda r, i: rb2.at[t, r - 1])
         s2[t] = (
@@ -569,44 +569,39 @@
             slot = 1 + 4 * 9 + t * 3 + r - 1
             arrived(full.at[full_piece((at[t][0] - r + 4) % 4), cols(t)], rr.at[slot])
             share_piece(t, r)
+    out_own = pltpu.make_async_copy(full.at[own_half], full_hbm.at[own_half], sem_f.at[0])
+    out_own.start()
     adagrad_some(7, 8)
     for t in T3:
         for r in range(4):
             i = (at[t][0] - r + 4) % 4
             arrived(full.at[pl.ds(pl.multiple_of((1 - k) * 384 + i * 96, 32), 96), cols(t)], rr.at[46 + t * 4 + r])
-    out = pltpu.make_async_copy(full, full_hbm, sem_f)
-    out.start()
+    out_other = pltpu.make_async_copy(full.at[other_half], full_hbm.at[other_half], sem_f.at[1])
+    out_other.start()
     for n in range(CL):
         pltpu.make_async_copy(rows.at[n], new_hbm.at[pl.ds(n * LBL, LBL)], sem_o.at[n]).wait()
     drain()
-    out.wait()
-
-
-def finish(new_hbm, sums_ref, full_hbm, labels_hbm, acc_ref, grad_hbm, held, full, grad, sem_in, sem_out, sem_f, sem_g):
+    out_own.wait()
+    out_other.wait()
+
+
+def finish(new_hbm, sums_ref, full_ref, labels_hbm, acc_ref, grad_ref, held, sem_in, sem_out):
     parts = [pl.ds(n * LBL, LBL) for n in range(CL)]
-    bands = [pl.ds(n * 128, 128) for n in range(D // 128)]
-    loads = [pltpu.make_async_copy(full_hbm.at[b], full.at[b], sem_f.at[n]) for n, b in enumerate(bands)]
-    stores = [pltpu.make_async_copy(grad.at[b], grad_hbm.at[b], sem_g.at[n]) for n, b in enumerate(bands)]
     ins = [pltpu.make_async_copy(new_hbm.at[p], held.at[p], sem_in.at[n]) for n, p in enumerate(parts)]
     outs = [pltpu.make_async_copy(held.at[p], labels_hbm.at[p], sem_out.at[n]) for n, p in enumerate(parts)]
-    for copy in loads + ins:
+    for copy in ins:
         copy.start()
     acc_ref[...] = sums_ref[...]
     scale = 1.0 / math.sqrt(D)
-    squares = jnp.zeros((8, D), F32)
-    for n, b in enumerate(bands):
-        loads[n].wait()
-        wide = full[b, :].astype(F32)
-        squares = squares + jnp.sum((wide * wide).reshape(16, 8, D), axis=0)
+    wide = full_ref[...].astype(F32)
+    squares = jnp.sum(wide * wide, keepdims=True) * (scale * scale)
+    factor = jnp.minimum(1.0, D / jnp.sqrt(squares + 1e-06)) * scale
     for n in range(CL):
         ins[n].wait()
         outs[n].start()
-    squares = jnp.sum(squares, keepdims=True) * (scale * scale)
-    factor = jnp.minimum(1.0, D / jnp.sqrt(squares + 1e-06)) * scale
-    for n, b in enumerate(bands):
-        grad[b, :] = full[:, n * 128:(n + 1) * 128].astype(F32).T * factor
-        stores[n].start()
-    for copy in outs + stores:
+    for n in range(D // 128):
+        grad_ref[:, n * 128:(n + 1) * 128] = full_ref[n * 128:(n + 1) * 128, :].astype(F32).T * factor
+    for copy in outs:
         copy.wait()
 
 
@@ -646,7 +641,7 @@
             pltpu.VMEM((3, 3, 16, 128), BF),
             pltpu.VMEM((3, 12, 16, 128), BF),
             pltpu.VMEM((D, D), BF),
-            dma, dma((CL,)), dma,
+            dma, dma((CL,)), dma((2,)),
             dma((3, 10, 2, 2)), dma((3, 10, 2, 2)),
             dma((3, 3, 3)), dma((3, 3, 3)),
             dma((3, 4, 4)), dma((3, 4, 4)),
@@ -665,15 +660,9 @@
             jax.ShapeDtypeStruct((16, 128), F32),
             jax.ShapeDtypeStruct((D, D), F32),
         ),
-        in_specs=[hbm, vmem, hbm],
-        out_specs=(hbm, vmem, hbm),
-        scratch_shapes=[
-            pltpu.VMEM((CL * LBL, D), BF),
-            pltpu.VMEM((D, D), BF),
-            pltpu.VMEM((D, D), F32),
-            dma((CL,)), dma((CL,)), dma((D // 128,)), dma((D // 128,)),
-        ],
-        compiler_params=pltpu.CompilerParams(vmem_limit_bytes=63 * 1024 * 1024),
+        in_specs=[hbm, vmem, vmem],
+        out_specs=(hbm, vmem, vmem),
+        scratch_shapes=[pltpu.VMEM((CL * LBL, D), BF), dma((CL,)), dma((CL,))],
     )(new_labels, sums, proj)
     return labels_out, sums_out.reshape(-1), grad
 

time: 112 us -> 109 us (0.973)
  Pallas kernels: 111 us -> 108 us
    pallas_call x1, Pallas kernels: 105 us -> 103 us  [on_device(): pl.pallas_call(kernel, out_shape=(jax.ShapeDtypeStruct((CL * LBL, D), BF)...]
where the time goes in v4:
time: 109 us
  Pallas kernels  108 us (99%)
    pallas_call x1, Pallas kernels, on_device(): pl.pallas_call(kernel, out_shape=(jax.ShapeDtypeStruct((CL * LBL, D), BF)...  103 us
    pallas_call x1, Pallas kernels, on_device(): pl.pallas_call(finish, out_shape=(jax.ShapeDtypeStruct((CL * LBL, D), BF)...  5.48 us

profile of v4, /device:TPU:1, one launch (start us, length us, event | category | flops | bytes accessed | tf_op | source)
XLA Modules:
  0.0 109.1 jit_solution(11679023327549529926)
XLA Ops:
  0.6 102.8 %shard_map.85 = (bf16[2048,768]{1,0:T(8,128)(2,1)}, f32[16,128]{1,0:T(8,128)}, bf16[768,768]{1,0:T(8,128)(2,1)}) custom-call(bf16[128,768]{1,0:T(8,128)(2,1)} %q_ref.1, s32[32,128]{1,0:T(8,128)} %bitcast.4, s32[4,128]{1,0:T(4,128)} %bitcast.7, bf16[768,768]{1,0:T(8,128)(2,1)} %p_ref.1, f32[16,128]{1,0:T(8,128)} %bitcast.5, bf16[2048,768]{1,0:T(8,128)(2,1)} %l_hbm.1), custom_call_target="tpu_custom_call" | custom-call | flops 20000000000 | bytes 20000000 | tf_op jit(solution)/shard_map/pallas_call | solution.py:612
  103.5 5.5 %shard_map.86 = (bf16[2048,768]{1,0:T(8,128)(2,1)}, f32[16,128]{1,0:T(8,128)}, f32[768,768]{1,0:T(8,128)}) custom-call(bf16[2048,768]{1,0:T(8,128)(2,1)} %get-tuple-element.9.new_hbm, f32[16,128]{1,0:T(8,128)} %get-tuple-element.10.sums_ref, bf16[768,768]{1,0:T(8,128)(2,1)} %get-tuple-element.11.full_ref), custom_call_target="tpu_custom_call" | custom-call | tf_op jit(solution)/shard_map/pallas_call | solution.py:656

commit v5 on v4

--- a/solution.py
+++ b/solution.py
@@ -261,7 +261,7 @@
                 cp[pl.ds(pl.multiple_of(step * 4 * CL + u * CL, CL), CL), :] = jnp.concatenate(found, axis=0)
             return 0
 
-        lax.fori_loop(0, GROUP // 4, names, 0)
+        lax.fori_loop(0, GROUP // 4, names, 0, unroll=2)
         picked = cp[...] > 0.0
         rank = dot(jnp.where(picked, 1.0, 0.0).astype(BF), tri)
         cd[...] = jnp.where(picked, rank, -1.0)
@@ -291,7 +291,7 @@
                 )
             return 0
 
-        lax.fori_loop(0, GROUP // 4, hot, 0)
+        lax.fori_loop(0, GROUP // 4, hot, 0, unroll=2)
         for h in range(GROUP // 8):
             for n in range(CL):
                 line_marks = jnp.zeros((8, 128), F32)
@@ -345,7 +345,7 @@
             add(3)
             return 0
 
-        lax.fori_loop(0, CL // 4, cluster, 0)
+        lax.fori_loop(0, CL // 4, cluster, 0, unroll=2)
 
     def group_work(group):
         gather_rows(group)

time: 109 us -> 108 us (level)
    pallas_call x1, Pallas kernels: 103 us -> 101 us  [on_device(): pl.pallas_call(kernel, out_shape=(jax.ShapeDtypeStruct((CL * LBL, D), BF)...]
where the time goes in v5:
time: 108 us
  Pallas kernels  107 us (99%)
    pallas_call x1, Pallas kernels, on_device(): pl.pallas_call(kernel, out_shape=(jax.ShapeDtypeStruct((CL * LBL, D), BF)...  101 us
    pallas_call x1, Pallas kernels, on_device(): pl.pallas_call(finish, out_shape=(jax.ShapeDtypeStruct((CL * LBL, D), BF)...  5.48 us

profile of v5, /device:TPU:1, one launch (start us, length us, event | category | flops | bytes accessed | tf_op | source)
XLA Modules:
  0.0 107.8 jit_solution(12613214648434870024)
XLA Ops:
  0.6 101.5 %shard_map.85 = (bf16[2048,768]{1,0:T(8,128)(2,1)}, f32[16,128]{1,0:T(8,128)}, bf16[768,768]{1,0:T(8,128)(2,1)}) custom-call(bf16[128,768]{1,0:T(8,128)(2,1)} %q_ref.1, s32[32,128]{1,0:T(8,128)} %bitcast.4, s32[4,128]{1,0:T(4,128)} %bitcast.7, bf16[768,768]{1,0:T(8,128)(2,1)} %p_ref.1, f32[16,128]{1,0:T(8,128)} %bitcast.5, bf16[2048,768]{1,0:T(8,128)(2,1)} %l_hbm.1), custom_call_target="tpu_custom_call" | custom-call | flops 20000000000 | bytes 20000000 | tf_op jit(solution)/shard_map/pallas_call | solution.py:612
  102.1 5.5 %shard_map.86 = (bf16[2048,768]{1,0:T(8,128)(2,1)}, f32[16,128]{1,0:T(8,128)}, f32[768,768]{1,0:T(8,128)}) custom-call(bf16[2048,768]{1,0:T(8,128)(2,1)} %get-tuple-element.9.new_hbm, f32[16,128]{1,0:T(8,128)} %get-tuple-element.10.sums_ref, bf16[768,768]{1,0:T(8,128)(2,1)} %get-tuple-element.11.full_ref), custom_call_target="tpu_custom_call" | custom-call | tf_op jit(solution)/shard_map/pallas_call | solution.py:656
